TPU v7x, 32 devices: a whole 2x2x4 slice. The times are simulated.
32 devices in a mesh: sec: 8 (over z, y), ops: 4 (over x, core).
Axes of the slice: x: 2, y: 2, z: 4, core: 2. Of those that a mesh axis runs over, the one named last changes fastest.
Arguments:
- wavefunction: bfloat16 [32, 32, 256, 256], P('sec'), may hold values from -6 to 6
- left_ops: bfloat16 [8, 32, 256, 256], P('ops', 'sec'), may hold values from -0.375 to 0.375
- right_ops: bfloat16 [8, 32, 256, 256], P('ops', 'sec'), may hold values from -0.125 to 0.125
- left_sizes: int32 [32], replicated, may hold values from 64 to 256, as said below
- right_sizes: int32 [32], replicated, may hold values from 64 to 256, as said below
- links: int32 [32, 32], replicated, may hold values 0 or 1
Outputs:
- sigma: bfloat16 [32, 32, 256, 256], P('ops', 'sec')
Inputs may be any that keep to these rules, and one draw needn't show every extreme that they name: `left_sizes`: some sector has exactly 256 states. `right_sizes`: some sector has exactly 256 states.
All inputs are finite; a program needn't handle non-finite values.
Results may differ from a plain program's by a relative error of at most 0.005.
Values may be sent and summed in bfloat16 or wider, within the bound.
No kernel may reach another device: no remote copies, remote signals or barrier semaphores. Data moves between devices by JAX's collectives and lax.ppermute only.
A program may use at most 192 MiB of HBM per device.

v0:
```python
import jax
import jax.numpy as jnp
from jax import lax
from jax.sharding import PartitionSpec as P


def local(wavefunction, left_ops, right_ops, left_sizes, right_sizes, links):
    owned = wavefunction.shape[0]
    width = wavefunction.shape[2]
    first = lax.axis_index("sec") * owned
    states = jnp.arange(width, dtype=jnp.int32)
    left_mask = (states[None, :] < left_sizes[:, None]).astype(jnp.float32)
    right_mask = (states[None, :] < right_sizes[:, None]).astype(jnp.float32)
    links_wide = links.astype(jnp.float32)
    link_rows = lax.dynamic_slice_in_dim(links_wide, first, owned, 0)
    left_owned = lax.dynamic_slice_in_dim(left_mask, first, owned, 0)
    keep_left = (
        link_rows[:, :, None, None] * left_owned[:, None, :, None] * right_mask[None, :, None, :]
    )
    link_cols = lax.dynamic_slice_in_dim(links_wide, first, owned, 1)
    right_owned = lax.dynamic_slice_in_dim(right_mask, first, owned, 0)
    keep_right = (
        link_cols[:, :, None, None] * left_mask[:, None, :, None] * right_owned[None, :, None, :]
    )
    psi = jnp.where(keep_left > 0.0, wavefunction, jnp.zeros_like(wavefunction))
    psi_right = lax.all_to_all(psi, "sec", split_axis=1, concat_axis=0, tiled=True)
    full_left = lax.all_gather(left_ops, "sec", axis=1, tiled=True)
    upper = jnp.einsum(
        "kqab,qrbc->kqrac", full_left, psi_right, preferred_element_type=jnp.float32
    ).astype(jnp.bfloat16)
    total = jnp.einsum("kqrac,krdc->qrad", upper, right_ops, preferred_element_type=jnp.float32)
    summed = lax.psum_scatter(total, "ops", scatter_dimension=0, tiled=True)
    group_rows = summed.shape[0]
    keep_out = lax.dynamic_slice_in_dim(
        keep_right, lax.axis_index("ops") * group_rows, group_rows, 0
    )
    return (summed * keep_out).astype(jnp.bfloat16)


def solution(mesh):
    placed = (
        P("sec", None, None, None),
        P("ops", "sec", None, None),
        P("ops", "sec", None, None),
        P(),
        P(),
        P(),
    )
    return jax.shard_map(
        local, mesh=mesh, in_specs=placed, out_specs=P("ops", "sec", None, None), check_vma=False
    )
```

profile of v0, /device:TPU:9, one launch (start us, length us, event | category | flops | bytes accessed | tf_op | source)
XLA Modules:
  0.0 846.9 jit_solution(8855277800269656326)
XLA Ops:
  6.5 0.0 copy-start
  6.5 0.8 convert_element_type.26
  7.4 0.1 copy.20
  7.4 0.7 fusion.17
  8.2 0.7 fusion.18
  8.9 0.1 broadcast_multiply_fusion.1
  9.0 15.9 %fusion.3 = bf16[4,32,256,256]{3,2,0,1:T(8,128)(2,1)} fusion(bf16[4,32,256,256]{3,2,1,0:T(8,128)(2,1)} %param.6, f32[32,256]{1,0:T(8,128)S(1)} %fusion.18, f32[4,32,256]{2,0,1:T(4,128)S(1)} %broadcast_multiply_fusion.1), kind=kLoop, calls=%fused_computation.4 | loop fusion | flops 25165824 | bytes 33718272 | tf_op jit(solution)/shard_map/jit(_where)/select_n | solution.py:25
  24.9 0.0 copy-start.2
  24.9 5.9 all-to-all-start
  30.8 0.0 all-gather.2.cloned.1.call-start
  30.8 0.0 copy-done.2
  30.8 1.0 copy.24
  31.8 0.0 all-gather.2.cloned.1.call-update
  31.8 0.0 reduce-scatter.5.cloned.1.call-start
  31.9 460.0 %all-to-all-done = bf16[4,32,256,256]{3,2,0,1:T(8,128)(2,1)} async-done(((bf16[4,32,256,256]{3,2,0,1:T(8,128)(2,1)}), bf16[4,32,256,256]{3,2,0,1:T(8,128)(2,1)}, u32[]{:S(2)}, u32[]{:S(2)}) %all-to-all-start) | async-done | bytes 16777248 | tf_op jit(solution)/shard_map/all_to_all | solution.py:26
  491.9 13.9 %copy.23 = bf16[8,4,4,256,256]{4,3,2,1,0:T(8,128)(2,1)} copy(bf16[8,4,4,256,256]{4,3,1,2,0:T(8,128)(2,1)} %bitcast.2) | data formatting | bytes 33554432 | tf_op jit(solution)/shard_map/all_to_all | solution.py:26
  505.8 0.0 all-gather.2.cloned.1.call-done
  505.8 0.0 copy-done
  505.8 29.8 %fusion.8 = f32[32,4,256,256]{3,2,0,1:T(8,128)} fusion(bf16[32,4,256,256,1]{3,2,1,0,4:T(8,128)(2,1)} %bitcast.36, bf16[2,32,256,256]{3,2,0,1:T(8,128)(2,1)} %all-gather.2.cloned.1.call-done, bf16[2,4,256,256]{3,2,1,0:T(8,128)(2,1)S(1)} %copy-done), kind=kOutput, calls=%fused_computation.7 | convolution fusion | flops 17196646400 | bytes 59768832 | tf_op jit(solution)/shard_map/kqrac,krdc->qrad/dot_general | solution.py:31
  535.6 12.7 %copy.39 = f32[32,4,256,256]{3,2,1,0:T(8,128)S(1)} copy(f32[32,4,256,256]{3,2,0,1:T(8,128)} %fusion.8) | data formatting | bytes 67108864
  548.3 44.8 %copy.41 = f32[4,8,1024,256]{3,1,2,0:T(8,128)} copy(f32[4,8,1024,256]{3,2,1,0:T(8,128)S(1)} %bitcast.34) | data formatting | bytes 67108864
  593.1 0.0 reduce-scatter.5.cloned.1.call-update
  593.1 0.1 constant_dynamic-slice_fusion.2
  593.2 0.1 copy.28
  593.3 0.1 broadcast_multiply_fusion
  593.4 236.8 %reduce-scatter.5.cloned.1.call-done = f32[8,262144]{1,0:T(8,128)} async-done(((f32[32,262144]{1,0:T(8,128)}), f32[8,262144]{1,0:T(8,128)}) %reduce-scatter.5.cloned.1.call-update) | async-done | bytes 8388624
  830.1 0.0 copy-start.1
  830.1 6.2 copy.42
  836.3 1.4 fusion.13
  837.7 2.3 copy.29
  840.0 0.0 copy-done.1
  (4 shorter events, 0.0 us)
Async XLA Ops:
  6.5 499.2 %copy-start = (bf16[2,4,256,256]{3,2,1,0:T(8,128)(2,1)S(1)}, bf16[2,4,256,256]{3,2,1,0:T(8,128)(2,1)}, u32[]{:S(2)}) copy-start(bf16[2,4,256,256]{3,2,1,0:T(8,128)(2,1)} %param.8) | copy-start | bytes 3145732
  24.9 5.9 copy-start.2
  24.9 467.0 %all-to-all-start = ((bf16[4,32,256,256]{3,2,0,1:T(8,128)(2,1)}), bf16[4,32,256,256]{3,2,0,1:T(8,128)(2,1)}, u32[]{:S(2)}, u32[]{:S(2)}) async-start(bf16[4,32,256,256]{3,2,0,1:T(8,128)(2,1)} %fusion.3), calls=%async_computation | async-start | bytes 33554432 | tf_op jit(solution)/shard_map/all_to_all | solution.py:26
  30.8 475.0 %all-gather.2.cloned.1.call-start = ((), (), s32[]{:S(2)}) async-start(), calls=%async_computation.2 | async-start | bytes 9437184 | tf_op jit(solution)/shard_map/all_gather | solution.py:27
  31.8 798.3 %reduce-scatter.5.cloned.1.call-start = ((), (), s32[]{:S(2)}) async-start(), calls=%async_computation.3 | async-start | bytes 41943040
  830.1 9.9 %copy-start.1 = (bf16[2,4,256,256]{3,2,1,0:T(8,128)(2,1)S(1)}, bf16[2,4,256,256]{3,2,1,0:T(8,128)(2,1)}, u32[]{:S(2)}) copy-start(bf16[2,4,256,256]{3,2,1,0:T(8,128)(2,1)} %param.8) | copy-start | bytes 3145732
Sparse Core Ops, SparseCore 0:
  33.7 402.3 all-gather.1
  593.2 236.8 reduce-scatter.4
where the time goes:
time: 849 us; the launch traced here: 847 us
  waiting for transfers between devices  697 us (82%)
  local copies, waits for them, and re-layouts  81.2 us (10%)
  matrix products  29.8 us (4%)
  other arithmetic  19.8 us (2%)
  between operations  13.5 us (2%)
    all_to_all x1, waiting for transfers between devices, local(): lax.all_to_all(psi, 'sec', split_axis=1, concat_axis=0, tiled=True)  460 us
    unnamed x3, waiting for transfers between devices  237 us
    unnamed x10, local copies, waits for them, and re-layouts  64.7 us
    dot_general x1, matrix products, local(): jnp.einsum('kqrac,krdc->qrad', upper, right_ops, preferred_element_type=j...  29.8 us
  transfers between devices with their start and end apart: 3, of which 2 were waited for; matrix products, arithmetic and copies ran while one was open for 2% of the time, Pallas kernels for 0%

commit v1 on v0

--- a/solution.py
+++ b/solution.py
@@ -1,10 +1,16 @@
+import functools
+
 import jax
 import jax.numpy as jnp
 from jax import lax
-from jax.sharding import PartitionSpec as P
-
-
-def local(wavefunction, left_ops, right_ops, left_sizes, right_sizes, links):
+from jax.experimental import pallas as pl
+from jax.experimental.pallas import tpu as pltpu
+from jax.sharding import Mesh, PartitionSpec as P
+
+SPLITS = 2
+
+
+def generic(wavefunction, left_ops, right_ops, left_sizes, right_sizes, links):
     owned = wavefunction.shape[0]
     width = wavefunction.shape[2]
     first = lax.axis_index("sec") * owned
@@ -37,15 +43,182 @@
     return (summed * keep_out).astype(jnp.bfloat16)
 
 
+HEAD = 3
+
+
+def block_kernel(planes, cols, terms, start, s_ref, l_refs, p_refs, r_ref, out_ref):
+    f = pl.program_id(0)
+    i = pl.program_id(1) + start
+    z = s_ref[0]
+    o = s_ref[2]
+    sizes_at = HEAD + planes * 2 * cols
+    nr = s_ref[sizes_at + planes + f * cols + i]
+    width = out_ref.shape[-1]
+    groups = planes
+    per = terms // groups
+    for d in range(planes):
+        link = s_ref[HEAD + (d * 2 + f) * cols + i]
+        nq = s_ref[sizes_at + d]
+        slot = z ^ d
+
+        @pl.when(link > 0)
+        def _(d=d, nq=nq, slot=slot):
+            rows = lax.broadcasted_iota(jnp.int32, (width, width), 0)
+            lanes = lax.broadcasted_iota(jnp.int32, (width, width), 1)
+            keep = (rows < nq) & (lanes < nr)
+            psi = p_refs[d][0, 0]
+            psi = jnp.where(keep, psi.astype(jnp.float32), 0.0).astype(jnp.bfloat16)
+            total = jnp.zeros((width, width), jnp.float32)
+            for e in range(groups):
+                for kk in range(per):
+                    left = l_refs[d][(o ^ e) * per + kk]
+                    upper = jnp.dot(left, psi, preferred_element_type=jnp.float32)
+                    total += lax.dot_general(
+                        upper.astype(jnp.bfloat16),
+                        r_ref[0, e * per + kk, 0],
+                        (((1,), (1,)), ((), ())),
+                        preferred_element_type=jnp.float32,
+                    )
+            out_ref[0, slot, 0] = jnp.where(keep, total, 0.0).astype(out_ref.dtype)
+
+        @pl.when(link == 0)
+        def _(slot=slot):
+            out_ref[0, slot, 0] = jnp.zeros((width, width), out_ref.dtype)
+
+
+def multiply(scalars, lefts, psis, rights, start, count):
+    planes = len(lefts)
+    terms, width = lefts[0].shape[0], lefts[0].shape[-1]
+    cols = rights.shape[2]
+
+    def body(s_ref, *refs):
+        block_kernel(
+            planes, cols, terms, start, s_ref, refs[:planes], refs[planes : 2 * planes],
+            refs[2 * planes], refs[2 * planes + 1],
+        )
+
+    grid_spec = pltpu.PrefetchScalarGridSpec(
+        num_scalar_prefetch=1,
+        grid=(2, count),
+        in_specs=[pl.BlockSpec((terms, width, width), lambda f, i, s: (0, 0, 0))] * planes
+        + [pl.BlockSpec((1, 1, width, width), lambda f, i, s: (f ^ s[1], i + start, 0, 0))] * planes
+        + [pl.BlockSpec((1, terms, 1, width, width), lambda f, i, s: (f, 0, i + start, 0, 0))],
+        out_specs=pl.BlockSpec(
+            (1, planes, 1, width, width), lambda f, i, s: (f ^ s[1], 0, i, 0, 0)
+        ),
+    )
+    blocks = planes * 2 * count
+    return pl.pallas_call(
+        body,
+        grid_spec=grid_spec,
+        out_shape=jax.ShapeDtypeStruct((2, planes, count, width, width), jnp.bfloat16),
+        compiler_params=pltpu.CompilerParams(vmem_limit_bytes=40 * 2**20),
+        cost_estimate=pl.CostEstimate(
+            flops=blocks * terms * 4 * width**3 // 3,
+            bytes_accessed=(planes * terms + 2 * count * terms + 2 * blocks) * width * width * 2,
+            transcendentals=0,
+        ),
+    )(scalars, *lefts, *psis, rights)
+
+
+def planned(wavefunction, left_ops, right_ops, left_sizes, right_sizes, links):
+    planes = lax.axis_size("o")
+    z, y, o = lax.axis_index("z"), lax.axis_index("y"), lax.axis_index("o")
+    owned, sectors = wavefunction.shape[:2]
+    width = wavefunction.shape[-1]
+    half = planes // 2
+    plane_cols = sectors // planes
+    cols = plane_cols // 2
+
+    def along_z(value, pairs):
+        return lax.ppermute(value, "z", pairs)
+
+    def flip(value, axis, bit):
+        size = lax.axis_size(axis)
+        return lax.ppermute(value, axis, [(i, i ^ bit) for i in range(size)])
+
+    row = lax.dynamic_index_in_dim(wavefunction, o, 0, keepdims=False)
+
+    def columns_of(plane):
+        return lax.dynamic_slice_in_dim(row, plane * plane_cols, plane_cols, 0)
+
+    psis = [columns_of(z)]
+    for d in range(1, planes):
+        psis.append(
+            lax.ppermute(columns_of(z ^ d), "z", [(i, i ^ d) for i in range(planes)])
+        )
+    psis = [p.reshape(2, cols, width, width) for p in psis]
+
+    own = lax.all_to_all(left_ops, "o", split_axis=1, concat_axis=0, tiled=True)[:, 0]
+    beside = flip(own, "z", 1)
+    inner1 = along_z(own, [(1, 2), (2, 1)])
+    inner2 = along_z(beside, [(1, 2), (2, 1)])
+    outer1 = along_z(inner1, [(1, 0), (2, 3)])
+    outer2 = along_z(inner2, [(1, 0), (2, 3)])
+    inside = (z == 1) | (z == 2)
+    lefts = [own, beside, jnp.where(inside, inner2, outer1), jnp.where(inside, inner1, outer2)]
+
+    def swap_core(value):
+        return flip(value, "o", 1)
+
+    def swap_x(value):
+        return flip(value, "o", 2)
+
+    def swap_y(value):
+        return flip(value, "y", 1)
+
+    r_y = swap_y(right_ops)
+    r_x = swap_x(right_ops)
+    per = right_ops.shape[0]
+    r_xy = jnp.concatenate([swap_y(r_x[: per // 2]), swap_x(r_y[per // 2 :])], axis=0)
+    near = jnp.stack([right_ops, r_y])
+    far = jnp.stack([r_x, r_xy])
+    rights = jnp.concatenate([near, swap_core(near), far, swap_core(far)], axis=1)
+
+    q_of = ((z ^ jnp.arange(planes)) * 2 + y) * owned + o
+    r_of = (z * 2 + (y ^ jnp.arange(2)))[:, None] * cols + jnp.arange(cols)[None, :]
+    r_of = r_of.reshape(-1)
+    flags = (links[q_of][:, r_of] != 0).astype(jnp.int32)
+    scalars = jnp.concatenate(
+        [
+            jnp.stack([z, y, o]).astype(jnp.int32),
+            flags.reshape(-1),
+            left_sizes[q_of],
+            right_sizes[r_of],
+        ]
+    )
+
+    parts = []
+    count = cols // SPLITS
+    for part in range(SPLITS):
+        done = multiply(scalars, lefts, psis, rights, part * count, count)
+        done = done.reshape(2 * planes, count, width, width)
+        parts.append(
+            lax.all_to_all(done, ("y", "o"), split_axis=0, concat_axis=0, tiled=True)
+        )
+    return jnp.concatenate(parts, axis=1)
+
+
 def solution(mesh):
-    placed = (
-        P("sec", None, None, None),
-        P("ops", "sec", None, None),
-        P("ops", "sec", None, None),
-        P(),
-        P(),
-        P(),
-    )
-    return jax.shard_map(
-        local, mesh=mesh, in_specs=placed, out_specs=P("ops", "sec", None, None), check_vma=False
-    )
+    sec, ops = mesh.shape["sec"], mesh.shape["ops"]
+
+    def run(wavefunction, *rest):
+        sectors = wavefunction.shape[0]
+        if ops == 4 and sec == 2 * ops and sectors == sec * ops:
+            where = Mesh(mesh.devices.reshape(sec // 2, 2, ops), ("z", "y", "o"))
+            side, group, body = ("z", "y"), "o", planned
+        else:
+            where, side, group, body = mesh, "sec", "ops", generic
+        placed = (
+            P(side, None, None, None),
+            P(group, side, None, None),
+            P(group, side, None, None),
+            P(),
+            P(),
+            P(),
+        )
+        return jax.shard_map(
+            body, mesh=where, in_specs=placed, out_specs=P(group, side, None, None), check_vma=False
+        )(wavefunction, *rest)
+
+    return run

time: 849 us -> 258 us (0.30)
  waiting for transfers between devices: 697 us -> 121 us
  local copies, waits for them, and re-layouts: 81.2 us -> 19.3 us
  starting transfers between devices: 5.9 us -> 47.4 us
  blocking collectives: 0 us -> 32.6 us
  matrix products: 29.8 us -> 0 us
  Pallas kernels: 0 us -> 16.1 us
  between operations: 13.5 us -> 0.24 us
    all_to_all x1 -> x2, waiting for transfers between devices: 460 us -> 15.1 us  [the longest x1 7.97 us: planned(): lax.all_to_all(done, ('y', 'o'), split_axis=0, concat_axis=0, tiled=True)]
    unnamed x3 -> x0, waiting for transfers between devices: 237 us -> none
    ppermute x0 -> x14, waiting for transfers between devices: none -> 106 us  [the longest x4 67.9 us: along_z(): return lax.ppermute(value, 'z', pairs)]
    unnamed x10 -> x37, local copies, waits for them, and re-layouts: 64.7 us -> 10.9 us
    all_to_all x0 -> x1, blocking collectives: none -> 32.6 us  [planned(): lax.all_to_all(done, ('y', 'o'), split_axis=0, concat_axis=0, tiled=True)]
    dot_general x1 -> x0, matrix products: 29.8 us -> none  [local(): jnp.einsum('kqrac,krdc->qrad', upper, right_ops, preferred_element_type=j...]
    ppermute x0 -> x14, starting transfers between devices: none -> 26.1 us  [the longest x4 13.2 us: along_z(): return lax.ppermute(value, 'z', pairs)]
    pallas_call x0 -> x2, Pallas kernels: none -> 16.1 us  [multiply(): pl.pallas_call(body, grid_spec=grid_spec, out_shape=jax.ShapeDtypeStruct(...]
  transfers between devices with their start and end apart: 3 -> 16, of which waited for: 2 -> 9; matrix products, arithmetic and copies ran while one was open for 2% -> 10% of each run, Pallas kernels for 0% -> 3%
where the time goes in v1:
time: 258 us; the launch traced here: 257 us
  waiting for transfers between devices  121 us (47%)
  starting transfers between devices  47.4 us (18%)
  blocking collectives  32.6 us (13%)
  other arithmetic  19.7 us (8%)
  local copies, waits for them, and re-layouts  19.3 us (7%)
  Pallas kernels  16.1 us (6%)
    ppermute x4, waiting for transfers between devices, along_z(): return lax.ppermute(value, 'z', pairs)  67.9 us
    all_to_all x1, blocking collectives, planned(): lax.all_to_all(done, ('y', 'o'), split_axis=0, concat_axis=0, tiled=True)  32.6 us
    ppermute x3, waiting for transfers between devices, planned(): lax.ppermute(columns_of(z ^ d), 'z', [(i, i ^ d) for i in range(planes)])  21.4 us
    ppermute x7, waiting for transfers between devices, flip(): return lax.ppermute(value, axis, [(i, i ^ bit) for i in range(size)])  16.8 us
    all_to_all x1, starting transfers between devices, planned(): lax.all_to_all(done, ('y', 'o'), split_axis=0, concat_axis=0, tiled=True)  16.5 us
    pallas_call x2, Pallas kernels, multiply(): pl.pallas_call(body, grid_spec=grid_spec, out_shape=jax.ShapeDtypeStruct(...  16.1 us
    ppermute x4, starting transfers between devices, along_z(): return lax.ppermute(value, 'z', pairs)  13.2 us
    unnamed x37, local copies, waits for them, and re-layouts  10.9 us
  transfers between devices with their start and end apart: 16, of which 9 were waited for; matrix products, arithmetic and copies ran while one was open for 10% of the time, Pallas kernels for 3%

profile of v1, /device:TPU:9, one launch (start us, length us, event | category | flops | bytes accessed | tf_op | source)
XLA Modules:
  0.0 256.6 jit_solution(7463975729646598494)
XLA Ops:
  2.5 2.3 copy.15
  4.7 4.7 %all-to-all-start = ((bf16[2,4,256,256]{3,2,0,1:T(8,128)(2,1)}), bf16[2,4,256,256]{3,2,0,1:T(8,128)(2,1)S(1)}, u32[]{:S(2)}, u32[]{:S(2)}) async-start(bf16[2,4,256,256]{3,2,0,1:T(8,128)(2,1)} %copy.15), calls=%async_computation | async-start | bytes 2097152 | tf_op jit(solution)/shard_map/all_to_all | solution.py:152
  9.4 14.8 %collective-permute-done.10 = bf16[2,4,256,256]{3,2,1,0:T(8,128)(2,1)S(1)} collective-permute-done((bf16[2,4,256,256]{3,2,1,0:T(8,128)(2,1)}, bf16[2,4,256,256]{3,2,1,0:T(8,128)(2,1)S(1)}, u32[]{:S(2)}, u32[]{:S(2)}) %collective-permute-start.10) | collective-permute-done | bytes 1048608 | tf_op jit(solution)/shard_map/ppermute | solution.py:138
  28.5 7.1 %all-to-all-done = bf16[2,4,256,256]{3,2,0,1:T(8,128)(2,1)S(1)} async-done(((bf16[2,4,256,256]{3,2,0,1:T(8,128)(2,1)}), bf16[2,4,256,256]{3,2,0,1:T(8,128)(2,1)S(1)}, u32[]{:S(2)}, u32[]{:S(2)}) %all-to-all-start) | async-done | bytes 1048608 | tf_op jit(solution)/shard_map/all_to_all | solution.py:152
  35.6 3.2 %collective-permute-start.2 = (bf16[8,256,256]{2,1,0:T(8,128)(2,1)S(1)}, bf16[8,256,256]{2,1,0:T(8,128)(2,1)}, u32[]{:S(2)}, u32[]{:S(2)}) collective-permute-start(bf16[8,256,256]{2,1,0:T(8,128)(2,1)S(1)} %bitcast.33), channel_id=1, source_target_pairs={{8,16},{16,8},{9,17},{17,9},{10,18},{18,10},{11,19},{19,11},{12,20... | collective-permute-start | bytes 3145736 | tf_op jit(solution)/shard_map/ppermute | solution.py:134
  38.9 3.1 %pad_maximum_fusion.2 = bf16[2,2,4,256,256]{4,3,2,1,0:T(8,128)(2,1)} fusion(bf16[1,2,4,256,256]{4,3,2,1,0:T(8,128)(2,1)} %bitcast.45, bf16[1,2,4,256,256]{4,3,2,1,0:T(8,128)(2,1)} %bitcast.47), kind=kLoop, calls=%fused_computation.6 | loop fusion | flops 1048576 | bytes 4194304 | tf_op jit(solution)/shard_map/stack | solution.py:174
  41.9 2.9 %collective-permute-start.9 = (bf16[2,2,4,256,256]{4,3,2,1,0:T(8,128)(2,1)}, bf16[2,2,4,256,256]{4,3,2,1,0:T(8,128)(2,1)}, u32[]{:S(2)}, u32[]{:S(2)}) collective-permute-start(bf16[2,2,4,256,256]{4,3,2,1,0:T(8,128)(2,1)} %pad_maximum_fusion.2), channel_id=1, source_target_pairs={{0,1},{1,0},{2,3},{3,2},{4,5},{5,4},{6,7},{7,6},{8,9},{9,8},{10,11... | collective-permute-start | bytes 6291464 | tf_op jit(solution)/shard_map/ppermute | solution.py:138
  44.8 2.0 collective-permute-done.12
  46.8 1.3 maximum_bitcast_fusion
  49.2 1.5 pad_maximum_fusion.3
  50.7 1.5 collective-permute-start.13
  52.2 3.9 %dynamic-slice_bitcast_fusion = (bf16[8,256,256]{2,1,0:T(8,128)(2,1)}, bf16[8,256,256]{2,1,0:T(8,128)(2,1)}, bf16[1,8,256,256]{3,2,1,0:T(8,128)(2,1)S(1)}, bf16[8,256,256]{2,1,0:T(8,128)(2,1)}) fusion(bf16[4,32,256,256]{3,2,1,0:T(8,128)(2,1)} %param.6, s32[]{:T(128)S(6)} %select_n.66, s32[]{:T(128)S(6)} %select_n.74, s32[]{:T(128)S(6)} %select_n.70, ...), kind=kLoop, calls=%fused_computation.9 | loop fusion | bytes 8388628 | tf_op jit(solution)/shard_map/dynamic_slice | solution.py:143
  57.4 2.3 collective-permute-done.2
  59.6 2.8 %collective-permute-start.3 = (bf16[8,256,256]{2,1,0:T(8,128)(2,1)}, bf16[8,256,256]{2,1,0:T(8,128)(2,1)}, u32[]{:S(2)}, u32[]{:S(2)}) collective-permute-start(bf16[8,256,256]{2,1,0:T(8,128)(2,1)} %collective-permute-done.2), channel_id=1, source_target_pairs={{8,0},{16,24},{9,1},{17,25},{10,2},{18,26},{11,3},{19,27},{12,4},{... | collective-permute-start | bytes 3145736 | tf_op jit(solution)/shard_map/ppermute | solution.py:134
  62.5 2.6 %collective-permute-start.1 = (bf16[8,256,256]{2,1,0:T(8,128)(2,1)S(1)}, bf16[8,256,256]{2,1,0:T(8,128)(2,1)}, u32[]{:S(2)}, u32[]{:S(2)}) collective-permute-start(bf16[8,256,256]{2,1,0:T(8,128)(2,1)S(1)} %collective-permute-done.refs_1_), channel_id=1, source_target_pairs={{8,16},{16,8},{9,17},{17,9},{10,18},{18,10},{11,19},{19,11},{12,20... | collective-permute-start | bytes 3145736 | tf_op jit(solution)/shard_map/ppermute | solution.py:134
  68.1 32.1 %collective-permute-done.3 = bf16[8,256,256]{2,1,0:T(8,128)(2,1)} collective-permute-done((bf16[8,256,256]{2,1,0:T(8,128)(2,1)}, bf16[8,256,256]{2,1,0:T(8,128)(2,1)}, u32[]{:S(2)}, u32[]{:S(2)}) %collective-permute-start.3) | collective-permute-done | bytes 1048608 | tf_op jit(solution)/shard_map/ppermute | solution.py:134
  100.2 2.2 collective-permute-start.5
  102.4 24.6 %collective-permute-done.1 = bf16[8,256,256]{2,1,0:T(8,128)(2,1)} collective-permute-done((bf16[8,256,256]{2,1,0:T(8,128)(2,1)S(1)}, bf16[8,256,256]{2,1,0:T(8,128)(2,1)}, u32[]{:S(2)}, u32[]{:S(2)}) %collective-permute-start.1) | collective-permute-done | bytes 1048608 | tf_op jit(solution)/shard_map/ppermute | solution.py:134
  127.1 1.3 broadcast_select_fusion.1.refs_2_
  128.4 4.6 %collective-permute-start.4 = (bf16[8,256,256]{2,1,0:T(8,128)(2,1)}, bf16[8,256,256]{2,1,0:T(8,128)(2,1)S(1)}, u32[]{:S(2)}, u32[]{:S(2)}) collective-permute-start(bf16[8,256,256]{2,1,0:T(8,128)(2,1)} %collective-permute-done.1), channel_id=1, source_target_pairs={{8,0},{16,24},{9,1},{17,25},{10,2},{18,26},{11,3},{19,27},{12,4},{... | collective-permute-start | bytes 3145736 | tf_op jit(solution)/shard_map/ppermute | solution.py:134
  133.0 7.1 %pad_maximum_fusion.refs_8_ = bf16[2,8,4,256,256]{4,3,2,1,0:T(8,128)(2,1)} fusion(bf16[2,2,4,256,256]{4,3,2,1,0:T(8,128)(2,1)} %collective-permute-done.13, bf16[1,2,4,256,256]{4,3,2,1,0:T(8,128)(2,1)} %copy-done.15, bf16[1,2,4,256,256]{4,3,2,1,0:T(8,128)(2,1)} %bitcast.44, bf16[2,2,4,256,256]{4,3,2,1,0:T(8,128)(2,1)} %collective-permute-done.9, ...), kind=kLoop, calls=%fused_computation.4 | loop fusion | flops 20971520 | bytes 16777216 | tf_op jit(solution)/shard_map/concatenate | solution.py:176
  140.1 8.9 %collective-permute-done.4 = bf16[8,256,256]{2,1,0:T(8,128)(2,1)S(1)} collective-permute-done((bf16[8,256,256]{2,1,0:T(8,128)(2,1)}, bf16[8,256,256]{2,1,0:T(8,128)(2,1)S(1)}, u32[]{:S(2)}, u32[]{:S(2)}) %collective-permute-start.4) | collective-permute-done | bytes 1048608 | tf_op jit(solution)/shard_map/ppermute | solution.py:134
  149.1 1.3 broadcast_select_fusion.refs_3_
  150.4 21.4 %collective-permute-done.6 = bf16[8,256,256]{2,1,0:T(8,128)(2,1)S(1)} collective-permute-done((bf16[8,256,256]{2,1,0:T(8,128)(2,1)}, bf16[8,256,256]{2,1,0:T(8,128)(2,1)S(1)}, u32[]{:S(2)}, u32[]{:S(2)}) %collective-permute-start.6) | collective-permute-done | bytes 1048608 | tf_op jit(solution)/shard_map/ppermute | solution.py:148
  171.8 7.2 %shard_map.65 = bf16[2,4,2,256,256]{4,3,2,1,0:T(8,128)(2,1)S(1)} custom-call(s32[47]{0:T(128)S(1)} %concatenate.12.s_ref, bf16[8,256,256]{2,1,0:T(8,128)(2,1)S(1)} %bitcast.35, bf16[8,256,256]{2,1,0:T(8,128)(2,1)S(1)} %copy-done.7, bf16[8,256,256]{2,1,0:T(8,128)(2,1)S(1)} %broadcast_select_fusion.1.refs_2_, ...), custom_call_target="tpu_custom_call" | custom-call | flops 2863311616 | bytes 12582912 | tf_op jit(solution)/shard_map/pallas_call | solution.py:111
  179.0 1.3 copy-done.4
  180.3 16.5 %all-to-all-start.2 = ((bf16[8,2,256,256]{3,2,1,0:T(8,128)(2,1)}), bf16[8,2,256,256]{3,2,1,0:T(8,128)(2,1)}, u32[]{:S(2)}, u32[]{:S(2)}) async-start(bf16[8,2,256,256]{3,2,1,0:T(8,128)(2,1)} %bitcast.37), calls=%async_computation.2 | async-start | bytes 4194304 | tf_op jit(solution)/shard_map/all_to_all | solution.py:197
  201.8 8.9 %shard_map.64 = bf16[2,4,2,256,256]{4,3,2,1,0:T(8,128)(2,1)S(1)} custom-call(s32[47]{0:T(128)S(1)} %concatenate.12.s_ref, bf16[8,256,256]{2,1,0:T(8,128)(2,1)S(1)} %bitcast.36, bf16[8,256,256]{2,1,0:T(8,128)(2,1)S(1)} %copy-done.8, bf16[8,256,256]{2,1,0:T(8,128)(2,1)S(1)} %broadcast_select_fusion.1.refs_2_, bf16[8,256,256]{2,1,0:T(8,128)(2,1)S(1)} %copy-done.3, ...), custom_call_target="tpu_custom_call" | custom-call | flops 2863311616 | bytes 12582912 | tf_op jit(solution)/shard_map/pallas_call | solution.py:111
  210.7 1.3 copy-done.5
  212.1 8.0 %all-to-all-done.2 = bf16[8,2,256,256]{3,2,1,0:T(8,128)(2,1)} async-done(((bf16[8,2,256,256]{3,2,1,0:T(8,128)(2,1)}), bf16[8,2,256,256]{3,2,1,0:T(8,128)(2,1)}, u32[]{:S(2)}, u32[]{:S(2)}) %all-to-all-start.2) | async-done | bytes 2097184 | tf_op jit(solution)/shard_map/all_to_all | solution.py:197
  220.0 32.6 %all_to_all.25 = bf16[8,2,256,256]{3,2,1,0:T(8,128)(2,1)S(1)} all-to-all(bf16[8,2,256,256]{3,2,1,0:T(8,128)(2,1)} %bitcast.38), channel_id=1, replica_groups=mesh['z'=4,'y'=2,'o'=4] {'y','o'}, dimensions={0} | all-to-all | bytes 4194304 | tf_op jit(solution)/shard_map/all_to_all | solution.py:197
  252.6 4.0 %pad_maximum_fusion.1 = bf16[8,4,256,256]{3,2,1,0:T(8,128)(2,1)} fusion(bf16[8,2,256,256]{3,2,1,0:T(8,128)(2,1)} %all-to-all-done.2, bf16[8,2,256,256]{3,2,1,0:T(8,128)(2,1)S(1)} %all_to_all.25), kind=kLoop, calls=%fused_computation.5 | loop fusion | flops 2097152 | bytes 8388608 | tf_op jit(solution)/shard_map/concatenate | solution.py:199
  (66 shorter events, 17.0 us)
Async XLA Ops:
  0.0 66.0 %copy-start = (s32[32,32]{1,0:T(8,128)S(1)}, s32[32,32]{1,0:T(8,128)}, u32[]{:S(2)}) copy-start(s32[32,32]{1,0:T(8,128)} %param.11) | copy-start | bytes 12292
  0.0 24.2 %collective-permute-start.10 = (bf16[2,4,256,256]{3,2,1,0:T(8,128)(2,1)}, bf16[2,4,256,256]{3,2,1,0:T(8,128)(2,1)S(1)}, u32[]{:S(2)}, u32[]{:S(2)}) collective-permute-start(bf16[2,4,256,256]{3,2,1,0:T(8,128)(2,1)} %param.8), channel_id=1, source_target_pairs={{0,2},{1,3},{2,0},{3,1},{4,6},{5,7},{6,4},{7,5},{8,10},{9,11},{10,... | collective-permute-start | bytes 3145736 | tf_op jit(solution)/shard_map/ppermute | solution.py:138
  1.2 25.2 %collective-permute-start.8 = (bf16[2,4,256,256]{3,2,1,0:T(8,128)(2,1)}, bf16[2,4,256,256]{3,2,1,0:T(8,128)(2,1)S(1)}, u32[]{:S(2)}, u32[]{:S(2)}) collective-permute-start(bf16[2,4,256,256]{3,2,1,0:T(8,128)(2,1)} %param.8), channel_id=1, source_target_pairs={{0,4},{4,0},{1,5},{5,1},{2,6},{6,2},{3,7},{7,3},{8,12},{12,8},{9,1... | collective-permute-start | bytes 3145736 | tf_op jit(solution)/shard_map/ppermute | solution.py:138
  4.7 30.9 %all-to-all-start = ((bf16[2,4,256,256]{3,2,0,1:T(8,128)(2,1)}), bf16[2,4,256,256]{3,2,0,1:T(8,128)(2,1)S(1)}, u32[]{:S(2)}, u32[]{:S(2)}) async-start(bf16[2,4,256,256]{3,2,0,1:T(8,128)(2,1)} %copy.15), calls=%async_computation | async-start | bytes 2097152 | tf_op jit(solution)/shard_map/all_to_all | solution.py:152
  24.2 23.9 %copy-start.16 = (bf16[2,4,256,256]{3,2,1,0:T(8,128)(2,1)}, bf16[2,4,256,256]{3,2,1,0:T(8,128)(2,1)S(1)}, u32[]{:S(2)}) copy-start(bf16[2,4,256,256]{3,2,1,0:T(8,128)(2,1)S(1)} %collective-permute-done.10) | copy-start | bytes 3145732
  25.1 19.7 %collective-permute-start.11 = (bf16[1,4,256,256]{3,2,1,0:T(8,128)(2,1)}, bf16[1,4,256,256]{3,2,1,0:T(8,128)(2,1)}, u32[]{:S(2)}, u32[]{:S(2)}) collective-permute-start(bf16[1,4,256,256]{3,2,1,0:T(8,128)(2,1)} %slice.16), channel_id=1, source_target_pairs={{0,4},{4,0},{1,5},{5,1},{2,6},{6,2},{3,7},{7,3},{8,12},{12,8},{9,1... | collective-permute-start | bytes 1572872 | tf_op jit(solution)/shard_map/ppermute | solution.py:138
  26.4 9.2 %copy-start.17 = (bf16[2,4,256,256]{3,2,1,0:T(8,128)(2,1)}, bf16[2,4,256,256]{3,2,1,0:T(8,128)(2,1)S(1)}, u32[]{:S(2)}) copy-start(bf16[2,4,256,256]{3,2,1,0:T(8,128)(2,1)S(1)} %collective-permute-done.8) | copy-start | bytes 3145732
  27.3 19.6 %collective-permute-start.12 = (bf16[1,4,256,256]{3,2,1,0:T(8,128)(2,1)}, bf16[1,4,256,256]{3,2,1,0:T(8,128)(2,1)}, u32[]{:S(2)}, u32[]{:S(2)}) collective-permute-start(bf16[1,4,256,256]{3,2,1,0:T(8,128)(2,1)} %slice.17), channel_id=1, source_target_pairs={{0,2},{1,3},{2,0},{3,1},{4,6},{5,7},{6,4},{7,5},{8,10},{9,11},{10,... | collective-permute-start | bytes 1572872 | tf_op jit(solution)/shard_map/ppermute | solution.py:138
  35.6 24.1 %collective-permute-start.2 = (bf16[8,256,256]{2,1,0:T(8,128)(2,1)S(1)}, bf16[8,256,256]{2,1,0:T(8,128)(2,1)}, u32[]{:S(2)}, u32[]{:S(2)}) collective-permute-start(bf16[8,256,256]{2,1,0:T(8,128)(2,1)S(1)} %bitcast.33), channel_id=1, source_target_pairs={{8,16},{16,8},{9,17},{17,9},{10,18},{18,10},{11,19},{19,11},{12,20... | collective-permute-start | bytes 3145736 | tf_op jit(solution)/shard_map/ppermute | solution.py:134
  38.8 23.7 %collective-permute-start = (bf16[8,256,256]{2,1,0:T(8,128)(2,1)S(1)}, bf16[8,256,256]{2,1,0:T(8,128)(2,1)S(1)}, u32[]{:S(2)}, u32[]{:S(2)}) collective-permute-start(bf16[8,256,256]{2,1,0:T(8,128)(2,1)S(1)} %bitcast.34), channel_id=1, source_target_pairs={{0,8},{8,0},{16,24},{24,16},{1,9},{9,1},{17,25},{25,17},{2,10},{10... | collective-permute-start | bytes 3145736 | tf_op jit(solution)/shard_map/ppermute | solution.py:138
  41.9 86.5 %collective-permute-start.9 = (bf16[2,2,4,256,256]{4,3,2,1,0:T(8,128)(2,1)}, bf16[2,2,4,256,256]{4,3,2,1,0:T(8,128)(2,1)}, u32[]{:S(2)}, u32[]{:S(2)}) collective-permute-start(bf16[2,2,4,256,256]{4,3,2,1,0:T(8,128)(2,1)} %pad_maximum_fusion.2), channel_id=1, source_target_pairs={{0,1},{1,0},{2,3},{3,2},{4,5},{5,4},{6,7},{7,6},{8,9},{9,8},{10,11... | collective-permute-start | bytes 6291464 | tf_op jit(solution)/shard_map/ppermute | solution.py:138
  50.7 82.4 %collective-permute-start.13 = (bf16[2,2,4,256,256]{4,3,2,1,0:T(8,128)(2,1)}, bf16[2,2,4,256,256]{4,3,2,1,0:T(8,128)(2,1)}, u32[]{:S(2)}, u32[]{:S(2)}) collective-permute-start(bf16[2,2,4,256,256]{4,3,2,1,0:T(8,128)(2,1)} %pad_maximum_fusion.3), channel_id=1, source_target_pairs={{0,1},{1,0},{2,3},{3,2},{4,5},{5,4},{6,7},{7,6},{8,9},{9,8},{10,11... | collective-permute-start | bytes 6291464 | tf_op jit(solution)/shard_map/ppermute | solution.py:138
  52.2 13.1 %copy-start.13 = (s32[32]{0:T(128)S(1)}, s32[32]{0:T(128)}, u32[]{:S(2)}) copy-start(s32[32]{0:T(128)} %param.9) | copy-start | bytes 388
  52.2 14.4 %copy-start.14 = (s32[32]{0:T(128)S(1)}, s32[32]{0:T(128)}, u32[]{:S(2)}) copy-start(s32[32]{0:T(128)} %param.10) | copy-start | bytes 388
  56.1 94.3 %collective-permute-start.7 = (bf16[8,256,256]{2,1,0:T(8,128)(2,1)}, bf16[8,256,256]{2,1,0:T(8,128)(2,1)}, u32[]{:S(2)}, u32[]{:S(2)}) collective-permute-start(bf16[8,256,256]{2,1,0:T(8,128)(2,1)} %get-tuple-element.5), channel_id=1, source_target_pairs={{0,24},{8,16},{16,8},{24,0},{1,25},{9,17},{17,9},{25,1},{2,26},{10... | collective-permute-start | bytes 3145736 | tf_op jit(solution)/shard_map/ppermute | solution.py:148
  59.6 40.6 %collective-permute-start.3 = (bf16[8,256,256]{2,1,0:T(8,128)(2,1)}, bf16[8,256,256]{2,1,0:T(8,128)(2,1)}, u32[]{:S(2)}, u32[]{:S(2)}) collective-permute-start(bf16[8,256,256]{2,1,0:T(8,128)(2,1)} %collective-permute-done.2), channel_id=1, source_target_pairs={{8,0},{16,24},{9,1},{17,25},{10,2},{18,26},{11,3},{19,27},{12,4},{... | collective-permute-start | bytes 3145736 | tf_op jit(solution)/shard_map/ppermute | solution.py:134
  62.5 64.6 %copy-start.6 = (bf16[8,256,256]{2,1,0:T(8,128)(2,1)}, bf16[8,256,256]{2,1,0:T(8,128)(2,1)S(1)}, u32[]{:S(2)}) copy-start(bf16[8,256,256]{2,1,0:T(8,128)(2,1)S(1)} %collective-permute-done.refs_1_) | copy-start | bytes 3145732
  62.5 64.6 %collective-permute-start.1 = (bf16[8,256,256]{2,1,0:T(8,128)(2,1)S(1)}, bf16[8,256,256]{2,1,0:T(8,128)(2,1)}, u32[]{:S(2)}, u32[]{:S(2)}) collective-permute-start(bf16[8,256,256]{2,1,0:T(8,128)(2,1)S(1)} %collective-permute-done.refs_1_), channel_id=1, source_target_pairs={{8,16},{16,8},{9,17},{17,9},{10,18},{18,10},{11,19},{19,11},{12,20... | collective-permute-start | bytes 3145736 | tf_op jit(solution)/shard_map/ppermute | solution.py:134
  100.2 50.2 %collective-permute-start.5 = (bf16[8,256,256]{2,1,0:T(8,128)(2,1)}, bf16[8,256,256]{2,1,0:T(8,128)(2,1)S(1)}, u32[]{:S(2)}, u32[]{:S(2)}) collective-permute-start(bf16[8,256,256]{2,1,0:T(8,128)(2,1)} %get-tuple-element.6), channel_id=1, source_target_pairs={{0,8},{8,0},{16,24},{24,16},{1,9},{9,1},{17,25},{25,17},{2,10},{10... | collective-permute-start | bytes 3145736 | tf_op jit(solution)/shard_map/ppermute | solution.py:148
  127.1 44.7 %collective-permute-start.6 = (bf16[8,256,256]{2,1,0:T(8,128)(2,1)}, bf16[8,256,256]{2,1,0:T(8,128)(2,1)S(1)}, u32[]{:S(2)}, u32[]{:S(2)}) collective-permute-start(bf16[8,256,256]{2,1,0:T(8,128)(2,1)} %get-tuple-element.8), channel_id=1, source_target_pairs={{0,16},{8,24},{16,0},{24,8},{1,17},{9,25},{17,1},{25,9},{2,18},{10... | collective-permute-start | bytes 3145736 | tf_op jit(solution)/shard_map/ppermute | solution.py:148
  128.4 43.4 %copy-start.7 = (bf16[8,256,256]{2,1,0:T(8,128)(2,1)S(1)}, bf16[8,256,256]{2,1,0:T(8,128)(2,1)}, u32[]{:S(2)}) copy-start(bf16[8,256,256]{2,1,0:T(8,128)(2,1)} %copy-done.6) | copy-start | bytes 3145732
  128.4 20.6 %collective-permute-start.4 = (bf16[8,256,256]{2,1,0:T(8,128)(2,1)}, bf16[8,256,256]{2,1,0:T(8,128)(2,1)S(1)}, u32[]{:S(2)}, u32[]{:S(2)}) collective-permute-start(bf16[8,256,256]{2,1,0:T(8,128)(2,1)} %collective-permute-done.1), channel_id=1, source_target_pairs={{8,0},{16,24},{9,1},{17,25},{10,2},{18,26},{11,3},{19,27},{12,4},{... | collective-permute-start | bytes 3145736 | tf_op jit(solution)/shard_map/ppermute | solution.py:134
  150.4 28.6 %copy-start.2 = (bf16[8,256,256]{2,1,0:T(8,128)(2,1)}, bf16[8,256,256]{2,1,0:T(8,128)(2,1)S(1)}, u32[]{:S(2)}) copy-start(bf16[8,256,256]{2,1,0:T(8,128)(2,1)S(1)} %broadcast_select_fusion.refs_3_) | copy-start | bytes 3145732
  150.4 28.6 %copy-start.9 = (bf16[8,256,256]{2,1,0:T(8,128)(2,1)}, bf16[8,256,256]{2,1,0:T(8,128)(2,1)S(1)}, u32[]{:S(2)}) copy-start(bf16[8,256,256]{2,1,0:T(8,128)(2,1)S(1)} %collective-permute-done.5) | copy-start | bytes 3145732
  171.8 7.2 %copy-start.11 = (bf16[8,256,256]{2,1,0:T(8,128)(2,1)}, bf16[8,256,256]{2,1,0:T(8,128)(2,1)S(1)}, u32[]{:S(2)}) copy-start(bf16[8,256,256]{2,1,0:T(8,128)(2,1)S(1)} %collective-permute-done.6) | copy-start | bytes 3145732
  179.0 1.3 copy-start.4
  180.3 39.7 %all-to-all-start.2 = ((bf16[8,2,256,256]{3,2,1,0:T(8,128)(2,1)}), bf16[8,2,256,256]{3,2,1,0:T(8,128)(2,1)}, u32[]{:S(2)}, u32[]{:S(2)}) async-start(bf16[8,2,256,256]{3,2,1,0:T(8,128)(2,1)} %bitcast.37), calls=%async_computation.2 | async-start | bytes 4194304 | tf_op jit(solution)/shard_map/all_to_all | solution.py:197
  196.9 1.2 copy-start.3
  198.1 1.2 copy-start.8
  199.3 1.2 copy-start.10
  210.7 1.3 copy-start.5
  220.0 36.5 %copy-start.1 = (s32[32,32]{1,0:T(8,128)S(1)}, s32[32,32]{1,0:T(8,128)}, u32[]{:S(2)}) copy-start(s32[32,32]{1,0:T(8,128)} %param.11) | copy-start | bytes 12292
  (2 other events, 2.3 us)

commit v2 on v0

--- a/solution.py
+++ b/solution.py
@@ -1,10 +1,13 @@
+import functools
+
 import jax
 import jax.numpy as jnp
 from jax import lax
-from jax.sharding import PartitionSpec as P
-
-
-def local(wavefunction, left_ops, right_ops, left_sizes, right_sizes, links):
+from jax.experimental import pallas as pl
+from jax.experimental.pallas import tpu as pltpu
+from jax.sharding import Mesh, PartitionSpec as P
+
+def generic(wavefunction, left_ops, right_ops, left_sizes, right_sizes, links):
     owned = wavefunction.shape[0]
     width = wavefunction.shape[2]
     first = lax.axis_index("sec") * owned
@@ -37,15 +40,343 @@
     return (summed * keep_out).astype(jnp.bfloat16)
 
 
+HEAD = 4
+GROUPS = ((0, 2), (1, 3))
+
+
+def block_kernel(
+    group, planes, cols, terms, pieces, slots_at, s_ref, l_refs, p_refs, r_refs, out_ref
+):
+    f = pl.program_id(0)
+    i = pl.program_id(1)
+    z = s_ref[0]
+    sizes_at = HEAD + planes * 2 * cols
+    nr = s_ref[sizes_at + planes + f * cols + i]
+    width = out_ref.shape[-1]
+    per = terms // planes
+    for at, d in enumerate(group):
+        link = s_ref[HEAD + (d * 2 + f) * cols + i]
+        nq = s_ref[sizes_at + d]
+        slot = (z ^ d) // 2
+
+        @pl.when(link > 0)
+        def _(at=at, d=d, nq=nq, slot=slot):
+            rows = lax.broadcasted_iota(jnp.int32, (width, width), 0)
+            lanes = lax.broadcasted_iota(jnp.int32, (width, width), 1)
+            keep = (rows < nq) & (lanes < nr)
+            if pieces[d] == [None]:
+                psi = p_refs[at][0][0, 0]
+            else:
+                psi = p_refs[at][0][0]
+                for (_, first, _), ref in zip(pieces[d][1:], p_refs[at][1:]):
+                    held = s_ref[slots_at + (d * 2 + f) * cols + i] >= first
+                    psi = jnp.where(held, ref[0], psi)
+            psi = jnp.where(keep, psi.astype(jnp.float32), 0.0).astype(jnp.bfloat16)
+            total = jnp.zeros((width, width), jnp.float32)
+            for e in range(planes):
+                for kk in range(per):
+                    left = l_refs[at][e * per + kk]
+                    upper = jnp.dot(left, psi, preferred_element_type=jnp.float32)
+                    total += lax.dot_general(
+                        upper.astype(jnp.bfloat16),
+                        r_refs[e % 2][0, e // 2, kk, 0],
+                        (((1,), (1,)), ((), ())),
+                        preferred_element_type=jnp.float32,
+                    )
+            out_ref[0, slot, 0] = jnp.where(keep, total, 0.0).astype(out_ref.dtype)
+
+        @pl.when(link == 0)
+        def _(slot=slot):
+            out_ref[0, slot, 0] = jnp.zeros((width, width), out_ref.dtype)
+
+
+def multiply(group, room, scalars, lefts, psis, rights):
+    terms, width = lefts[0].shape[0], lefts[0].shape[-1]
+    cols = rights[0].shape[3]
+    per = rights[0].shape[2]
+    many = len(group)
+    planes = terms // per
+
+    slots_at = HEAD + planes * 2 * cols + planes + 2 * cols
+    pieces = {d: [piece for piece in ranges(room) if piece[0] == d] or [None] for d in group}
+
+    def body(s_ref, *refs):
+        l_refs, p_refs, at = refs[:many], [], many
+        for d in group:
+            p_refs.append(refs[at : at + len(pieces[d])])
+            at += len(pieces[d])
+        block_kernel(
+            group, planes, cols, terms, pieces, slots_at, s_ref, l_refs, p_refs,
+            refs[at:-1], refs[-1],
+        )
+
+    def psi_spec(d, piece):
+        if piece is None:
+            return pl.BlockSpec(
+                (1, 1, width, width),
+                lambda f, i, s: (s[2] * 2 + s[3], (s[0] * 2 + (f ^ s[1])) * cols + i, 0, 0),
+            )
+        _, first, count = piece
+
+        def index(f, i, s):
+            slot = s[slots_at + (d * 2 + f) * cols + i]
+            return (jnp.clip(slot - first, 0, count - 1), 0, 0)
+
+        return pl.BlockSpec((1, width, width), index)
+
+    grid_spec = pltpu.PrefetchScalarGridSpec(
+        num_scalar_prefetch=1,
+        grid=(2, cols),
+        in_specs=[pl.BlockSpec((terms, width, width), lambda f, i, s: (0, 0, 0))] * many
+        + [psi_spec(d, piece) for d in group for piece in pieces[d]]
+        + [
+            pl.BlockSpec((1, 2, per, 1, width, width), lambda f, i, s: (f, 0, 0, i, 0, 0))
+        ]
+        * 2,
+        out_specs=pl.BlockSpec((1, 2, 1, width, width), lambda f, i, s: (f ^ s[1], 0, i, 0, 0)),
+    )
+    blocks = many * 2 * cols
+    return pl.pallas_call(
+        body,
+        grid_spec=grid_spec,
+        out_shape=jax.ShapeDtypeStruct((2, 2, cols, width, width), jnp.bfloat16),
+        compiler_params=pltpu.CompilerParams(vmem_limit_bytes=48 * 2**20),
+        cost_estimate=pl.CostEstimate(
+            flops=blocks * terms * 4 * width**3 // 3,
+            bytes_accessed=(many * terms + 2 * cols * terms + 2 * blocks) * width * width * 2,
+            transcendentals=0,
+        ),
+    )(scalars, *lefts, *[piece for psi in psis for piece in psi], *rights)
+
+
+def put_together(place, own_core, other_core):
+    many, cols, width = own_core[0].shape[0], own_core[0].shape[1], own_core[0].shape[-1]
+
+    def body(s_ref, *refs):
+        out_ref = refs[-1]
+        first = (s_ref[0] + s_ref[3]) % 2 == 0
+        for at, mine in ((0, first), (1, jnp.logical_not(first))):
+
+            @pl.when(mine)
+            def _(at=at):
+                out_ref[0, s_ref[3]] = refs[at][0]
+                out_ref[0, 1 - s_ref[3]] = refs[2 + at][0]
+
+    def block_of(at):
+        def index(t, s):
+            return (jnp.where((s[0] + s[3]) % 2 == at, t, 0), 0, 0, 0)
+
+        return index
+
+    return pl.pallas_call(
+        body,
+        grid_spec=pltpu.PrefetchScalarGridSpec(
+            num_scalar_prefetch=1,
+            grid=(many,),
+            in_specs=[
+                pl.BlockSpec((1, cols, width, width), block_of(at)) for at in (0, 1, 0, 1)
+            ],
+            out_specs=pl.BlockSpec((1, 2, cols, width, width), lambda t, s: (t, 0, 0, 0, 0)),
+        ),
+        out_shape=jax.ShapeDtypeStruct((many, 2, cols, width, width), own_core[0].dtype),
+    )(place, *own_core, *other_core).reshape(2 * many, cols, width, width)
+
+
+PIECES = {1: 1, 2: 2, 3: 2}
+
+
+def ranges(room):
+    out = []
+    for d, many in PIECES.items():
+        ends = [-(-room * at // many) for at in range(many + 1)]
+        out += [(d, first, end - first) for first, end in zip(ends[:-1], ends[1:])]
+    return out
+
+
+def cut_out(cells, place, wavefunction, left_ops, planes, room):
+    width = wavefunction.shape[-1]
+    per = left_ops.shape[0]
+    pieces = ranges(room)
+    many = len(pieces)
+
+    def body(c_ref, s_ref, *refs):
+        half = len(refs) // 2
+        for at in range(many):
+            refs[half + at][0] = refs[at][0, 0]
+
+        @pl.when(pl.program_id(0) == 0)
+        def _():
+            for at in range(many, half):
+                refs[half + at][...] = refs[at][:, 0]
+
+    def block_of(d, first, count):
+        def index(t, c, s):
+            slot = first + jnp.minimum(t, count - 1)
+            return (s[2] * 2 + s[3], c[d * room + slot], 0, 0)
+
+        return index
+
+    def place_of(count):
+        return lambda t, c, s: (jnp.minimum(t, count - 1), 0, 0)
+
+    def sector_of(e):
+        return lambda t, c, s: (0, (s[2] * 2 + s[3]) ^ e, 0, 0)
+
+    outs = pl.pallas_call(
+        body,
+        grid_spec=pltpu.PrefetchScalarGridSpec(
+            num_scalar_prefetch=2,
+            grid=(max(count for _, _, count in pieces),),
+            in_specs=[pl.BlockSpec((1, 1, width, width), block_of(*piece)) for piece in pieces]
+            + [pl.BlockSpec((per, 1, width, width), sector_of(e)) for e in range(planes)],
+            out_specs=[pl.BlockSpec((1, width, width), place_of(count)) for _, _, count in pieces]
+            + [pl.BlockSpec((per, width, width), lambda t, c, s: (0, 0, 0))] * planes,
+        ),
+        out_shape=[
+            jax.ShapeDtypeStruct((count, width, width), wavefunction.dtype)
+            for _, _, count in pieces
+        ]
+        + [jax.ShapeDtypeStruct((per, width, width), left_ops.dtype)] * planes,
+    )(cells, place, *([wavefunction] * many), *([left_ops] * planes))
+    return outs[:many], outs[many:]
+
+
+def running(mask):
+    size = mask.shape[-1]
+    upto = jnp.arange(size)[:, None] >= jnp.arange(size)[None, :]
+    return jnp.sum(jnp.where(upto, mask[..., None, :], 0), axis=-1)
+
+
+def planned(room, place, cell_table, scalars, wavefunction, left_ops, right_ops):
+    planes = lax.axis_size("z")
+    z, y, x, c = (lax.axis_index(name) for name in ("z", "y", "x", "c"))
+    owned, sectors = wavefunction.shape[:2]
+    width = wavefunction.shape[-1]
+    cols = sectors // planes // 2
+    after = lax.optimization_barrier
+
+    def inner(value):
+        return lax.ppermute(value, "z", [(1, 2), (2, 1)])
+
+    def outer(value):
+        return lax.ppermute(value, "z", [(1, 0), (2, 3)])
+
+    def flip(value, axis, bit):
+        size = lax.axis_size(axis)
+        return lax.ppermute(value, axis, [(i, i ^ bit) for i in range(size)])
+
+    def on_ops(value, bit):
+        pairs = [(i, i ^ bit) for i in range(planes)]
+        return lax.ppermute(value, ("x", "c"), pairs)
+
+    cells = cell_table[:, :room].reshape(-1)
+    cuts, sectors_cut = cut_out(cells, place, wavefunction, left_ops, planes, room)
+    mine = [sectors_cut[0]] + [on_ops(sectors_cut[e], e) for e in range(1, planes)]
+    psis = {0: [wavefunction]}
+    for (d, _, _), cut in zip(ranges(room), cuts):
+        psis.setdefault(d, []).append(flip(cut, "z", d))
+    r_y = flip(right_ops, "y", 1)
+    r_x = flip(right_ops, "x", 1)
+    mine, r_x, r_y, psis[1], psis[2][0] = after((mine, r_x, r_y, psis[1], psis[2][0]))
+    per = right_ops.shape[0]
+    r_xy1 = flip(r_x[: per // 2], "y", 1)
+    r_xy2 = flip(r_y[per // 2 :], "x", 1)
+    own = jnp.concatenate(mine, axis=0)
+    beside = flip(own, "z", 1)
+    inner1 = inner(own)
+    beside, inner1, r_xy1, r_xy2, psis[2][1] = after((beside, inner1, r_xy1, r_xy2, psis[2][1]))
+    r_xy = jnp.concatenate([r_xy1, r_xy2], axis=0)
+    near = jnp.stack([right_ops, r_x, r_y, r_xy]).reshape(2, 2, *right_ops.shape)
+    other = flip(near, "c", 1)
+    inner2 = inner(beside)
+    outer1 = outer(inner1)
+    inner2, outer1, other, psis[3][0] = after((inner2, outer1, other, psis[3][0]))
+    rights = [near, other]
+    outer2 = outer(inner2)
+
+    inside = (z == 1) | (z == 2)
+    lefts = [own, beside, jnp.where(inside, inner2, outer1), jnp.where(inside, inner1, outer2)]
+
+    own_core, other_core = [], []
+    for group in GROUPS:
+        done = multiply(
+            group, room, scalars, [lefts[d] for d in group], [psis[d] for d in group], rights
+        )
+        done = done.reshape(4, cols, width, width)
+        own_core.append(
+            lax.all_to_all(done, ("y", "x"), split_axis=0, concat_axis=0, tiled=True)
+        )
+        other_core.append(flip(own_core[-1], "c", 1))
+    return put_together(place, own_core, other_core)
+
+
+def tables(wavefunction, left_sizes, right_sizes, links):
+    planes = lax.axis_size("z")
+    z, y, x, c = (lax.axis_index(name) for name in ("z", "y", "x", "c"))
+    owned, sectors = wavefunction.shape[:2]
+    plane_cols = sectors // planes
+    cols = plane_cols // 2
+    o = x * 2 + c
+    place = jnp.stack([z, y, x, c]).astype(jnp.int32)
+    flips = jnp.arange(planes)
+    marks = (links != 0).astype(jnp.int32)
+    by_row = marks.reshape(planes, 2, owned, planes, plane_cols)
+    away = (flips[:, None] != flips[None, :])[:, None, None, :]
+    most = jnp.max(jnp.where(away, jnp.sum(by_row, axis=-1), 0))
+
+    sent = marks[(z * 2 + y) * owned + o].reshape(planes, plane_cols)[z ^ flips]
+    slot = running(sent) - 1
+    hit = (slot[:, None, :] == jnp.arange(plane_cols)[None, :, None]) & (sent[:, None, :] > 0)
+    sector = (z ^ flips)[:, None] * plane_cols + jnp.arange(plane_cols)[None, :]
+    cell_table = jnp.sum(jnp.where(hit, sector[:, None, :], 0), axis=-1).astype(jnp.int32)
+
+    q_of = ((z ^ flips) * 2 + y) * owned + o
+    come = lax.dynamic_slice_in_dim(marks[q_of], z * plane_cols, plane_cols, 1)
+    slots = jnp.maximum(running(come) - 1, 0)
+
+    def sided(table):
+        table = table.reshape(planes, 2, cols)
+        return jnp.where(y > 0, table[:, ::-1], table).reshape(-1)
+
+    r_of = (z * 2 + (y ^ jnp.arange(2)))[:, None] * cols + jnp.arange(cols)[None, :]
+    scalars = jnp.concatenate(
+        [place, sided(come), left_sizes[q_of], right_sizes[r_of.reshape(-1)], sided(slots)]
+    ).astype(jnp.int32)
+    return most, place, cell_table, scalars
+
+
+ROOMS = (5, 6, 7)
+
+
+def sparse(wavefunction, left_ops, right_ops, left_sizes, right_sizes, links):
+    most, *rest = tables(wavefunction, left_sizes, right_sizes, links)
+    whole = wavefunction.shape[1] // lax.axis_size("z")
+    rooms = [room for room in ROOMS if room < whole] + [whole]
+    forms = [functools.partial(planned, room) for room in rooms]
+    which = jnp.sum((most > jnp.array(rooms[:-1], jnp.int32)).astype(jnp.int32))
+    return lax.switch(which, forms, *rest, wavefunction, left_ops, right_ops)
+
+
 def solution(mesh):
-    placed = (
-        P("sec", None, None, None),
-        P("ops", "sec", None, None),
-        P("ops", "sec", None, None),
-        P(),
-        P(),
-        P(),
-    )
-    return jax.shard_map(
-        local, mesh=mesh, in_specs=placed, out_specs=P("ops", "sec", None, None), check_vma=False
-    )
+    sec, ops = mesh.shape["sec"], mesh.shape["ops"]
+
+    def run(wavefunction, *rest):
+        sectors = wavefunction.shape[0]
+        if ops == 4 and sec == 2 * ops and sectors == sec * ops:
+            where = Mesh(mesh.devices.reshape(sec // 2, 2, ops // 2, 2), ("z", "y", "x", "c"))
+            side, group, body = ("z", "y"), ("x", "c"), sparse
+        else:
+            where, side, group, body = mesh, "sec", "ops", generic
+        placed = (
+            P(side, None, None, None),
+            P(group, side, None, None),
+            P(group, side, None, None),
+            P(),
+            P(),
+            P(),
+        )
+        return jax.shard_map(
+            body, mesh=where, in_specs=placed, out_specs=P(group, side, None, None), check_vma=False
+        )(wavefunction, *rest)
+
+    return run

time: 849 us -> 236 us (0.28)
  waiting for transfers between devices: 697 us -> 137 us
  local copies, waits for them, and re-layouts: 81.2 us -> 12.2 us
  starting transfers between devices: 5.9 us -> 45.6 us
  Pallas kernels: 0 us -> 32.3 us
  matrix products: 29.8 us -> 0 us
  between operations: 13.5 us -> 0.72 us
  other arithmetic: 19.8 us -> 10.4 us
    all_to_all x1 -> x2, waiting for transfers between devices: 460 us -> 24.8 us  [planned(): lax.all_to_all(done, ('y', 'x'), split_axis=0, concat_axis=0, tiled=True)]
    unnamed x3 -> x0, waiting for transfers between devices: 237 us -> none
    ppermute x0 -> x20, waiting for transfers between devices: none -> 112 us  [the longest x13 78.8 us: flip(): return lax.ppermute(value, axis, [(i, i ^ bit) for i in range(size)])]
    unnamed x10 -> x4, local copies, waits for them, and re-layouts: 64.7 us -> 0.99 us
    ppermute x0 -> x20, starting transfers between devices: none -> 33.8 us  [the longest x13 17.1 us: flip(): return lax.ppermute(value, axis, [(i, i ^ bit) for i in range(size)])]
    pallas_call x0 -> x4, Pallas kernels: none -> 32.3 us  [the longest x2 20 us: multiply(): pl.pallas_call(body, grid_spec=grid_spec, out_shape=jax.ShapeDtypeStruct(...]
    dot_general x1 -> x0, matrix products: 29.8 us -> none  [local(): jnp.einsum('kqrac,krdc->qrad', upper, right_ops, preferred_element_type=j...]
    all_to_all x1 -> x0, local copies, waits for them, and re-layouts: 13.9 us -> none  [local(): lax.all_to_all(psi, 'sec', split_axis=1, concat_axis=0, tiled=True)]
  transfers between devices with their start and end apart: 3 -> 22, of which waited for: 2 -> 10; matrix products, arithmetic and copies ran while one was open for 2% -> 3% of each run, Pallas kernels for 0% -> 11%
where the time goes in v2:
time: 236 us; the launch traced here: 238 us
  waiting for transfers between devices  137 us (58%)
  starting transfers between devices  45.6 us (19%)
  Pallas kernels  32.3 us (14%)
  local copies, waits for them, and re-layouts  12.2 us (5%)
  other arithmetic  10.4 us (4%)
    ppermute x13, waiting for transfers between devices, flip(): return lax.ppermute(value, axis, [(i, i ^ bit) for i in range(size)])  78.8 us
    all_to_all x2, waiting for transfers between devices, planned(): lax.all_to_all(done, ('y', 'x'), split_axis=0, concat_axis=0, tiled=True)  24.8 us
    ppermute x3, waiting for transfers between devices, on_ops(): return lax.ppermute(value, ('x', 'c'), pairs)  22.7 us
    pallas_call x2, Pallas kernels, multiply(): pl.pallas_call(body, grid_spec=grid_spec, out_shape=jax.ShapeDtypeStruct(...  20 us
    ppermute x13, starting transfers between devices, flip(): return lax.ppermute(value, axis, [(i, i ^ bit) for i in range(size)])  17.1 us
    all_to_all x2, starting transfers between devices, planned(): lax.all_to_all(done, ('y', 'x'), split_axis=0, concat_axis=0, tiled=True)  11.8 us
    ppermute x2, waiting for transfers between devices, outer(): return lax.ppermute(value, 'z', [(1, 0), (2, 3)])  10.2 us
    ppermute x2, starting transfers between devices, outer(): return lax.ppermute(value, 'z', [(1, 0), (2, 3)])  6.88 us
  transfers between devices with their start and end apart: 22, of which 10 were waited for; matrix products, arithmetic and copies ran while one was open for 3% of the time, Pallas kernels for 11%

profile of v2, /device:TPU:9, one launch (start us, length us, event | category | flops | bytes accessed | tf_op | source)
XLA Modules:
  0.0 238.2 jit_solution(7300340307843256269)
XLA Ops:
  1.3 1.3 gather_fusion.2
  6.7 2.0 fusion
  9.3 228.2 %conditional.1 = (bf16[8,4,256,256]{3,2,1,0:T(8,128)(2,1)}) conditional(s32[]{:T(128)} %clamp.3, (pred[4,8,8]{2,1,0:T(8,128)(4,1)S(1)}, s32[4]{0:T(128)S(1)}, bf16[4,32,256,256]{3,2,1,0:T(8,128)(2,1)}, bf16[2,4,256,256]{3,2,1,0:T(8,128)(2,1)}, bf16[2,4,256,256]{3,2,1,0:T(8,128)(2,1)}, /*index=5*/s32[80]{0:T(128)S(1)}, ...), branch_computations={%region_6.7_spmd, %region_7.8_spmd, %region_8.9_spmd, %region_9.10... | conditional | flops 5734489088 | bytes 185604160 | solution.py:357
  10.1 1.2 collective-permute-start.44
  14.2 6.7 %branch_2_fun.4 = (bf16[7,256,256]{2,1,0:T(8,128)(2,1)}, bf16[4,256,256]{2,1,0:T(8,128)(2,1)}, bf16[3,256,256]{2,1,0:T(8,128)(2,1)}, bf16[4,256,256]{2,1,0:T(8,1...) custom-call(s32[28]{0:T(128)} %reshape.176.c_ref, ...), custom_call_target="tpu_custom_call" | custom-call | tf_op jit(solution)/shard_map/cond/branch_2_fun/pallas_call | solution.py:225
  21.5 1.6 collective-permute-start.40
  23.1 1.4 collective-permute-done.40
  24.5 2.3 collective-permute-start.46
  26.8 14.0 %collective-permute-done.41 = bf16[2,256,256]{2,1,0:T(8,128)(2,1)S(1)} collective-permute-done((bf16[2,256,256]{2,1,0:T(8,128)(2,1)}, bf16[2,256,256]{2,1,0:T(8,128)(2,1)S(1)}, u32[]{:S(2)}, u32[]{:S(2)}) %collective-permute-start.41) | collective-permute-done | bytes 262176 | tf_op jit(solution)/shard_map/cond/branch_2_fun/ppermute | solution.py:270
  40.8 3.0 %collective-permute-start.42 = (bf16[2,256,256]{2,1,0:T(8,128)(2,1)}, bf16[2,256,256]{2,1,0:T(8,128)(2,1)S(1)}, u32[]{:S(2)}, u32[]{:S(2)}) collective-permute-start(bf16[2,256,256]{2,1,0:T(8,128)(2,1)} %get-tuple-element.130), channel_id=1, source_target_pairs={{0,3},{1,2},{2,1},{3,0},{4,7},{5,6},{6,5},{7,4},{8,11},{9,10},{10,... | collective-permute-start | bytes 786440 | tf_op jit(solution)/shard_map/cond/branch_2_fun/ppermute | solution.py:270
  43.8 7.3 %collective-permute-done.42 = bf16[2,256,256]{2,1,0:T(8,128)(2,1)S(1)} collective-permute-done((bf16[2,256,256]{2,1,0:T(8,128)(2,1)}, bf16[2,256,256]{2,1,0:T(8,128)(2,1)S(1)}, u32[]{:S(2)}, u32[]{:S(2)}) %collective-permute-start.42) | collective-permute-done | bytes 262176 | tf_op jit(solution)/shard_map/cond/branch_2_fun/ppermute | solution.py:270
  51.1 2.4 %collective-permute-done.46.refs_3_ = bf16[4,256,256]{2,1,0:T(8,128)(2,1)S(1)} collective-permute-done((bf16[4,256,256]{2,1,0:T(8,128)(2,1)}, bf16[4,256,256]{2,1,0:T(8,128)(2,1)S(1)}, u32[]{:S(2)}, u32[]{:S(2)}) %collective-permute-start.46) | collective-permute-done | bytes 524320 | tf_op jit(solution)/shard_map/cond/branch_2_fun/ppermute | solution.py:266
  55.7 2.6 %collective-permute-start.48 = (bf16[8,256,256]{2,1,0:T(8,128)(2,1)S(1)}, bf16[8,256,256]{2,1,0:T(8,128)(2,1)}, u32[]{:S(2)}, u32[]{:S(2)}) collective-permute-start(bf16[8,256,256]{2,1,0:T(8,128)(2,1)S(1)} %constant_dynamic-update-slice_fusion.8.refs_0_), channel_id=1, source_target_pairs={{8,16},{16,8},{9,17},{17,9},{10,18},{18,10},{11,19},{19,11},{12,20... | collective-permute-start | bytes 3145736 | tf_op jit(solution)/shard_map/cond/branch_2_fun/ppermute | solution.py:259
  61.7 2.5 %collective-permute-start.51 = (bf16[3,256,256]{2,1,0:T(8,128)(2,1)S(1)}, bf16[3,256,256]{2,1,0:T(8,128)(2,1)S(1)}, u32[]{:S(2)}, u32[]{:S(2)}) collective-permute-start(bf16[3,256,256]{2,1,0:T(8,128)(2,1)S(1)} %copy-done.48), channel_id=1, source_target_pairs={{0,16},{8,24},{16,0},{24,8},{1,17},{9,25},{17,1},{25,9},{2,18},{10... | collective-permute-start | bytes 1179656 | tf_op jit(solution)/shard_map/cond/branch_2_fun/ppermute | solution.py:266
  64.3 31.1 %collective-permute-done.51.refs_4_ = bf16[3,256,256]{2,1,0:T(8,128)(2,1)S(1)} collective-permute-done((bf16[3,256,256]{2,1,0:T(8,128)(2,1)S(1)}, bf16[3,256,256]{2,1,0:T(8,128)(2,1)S(1)}, u32[]{:S(2)}, u32[]{:S(2)}) %collective-permute-start.51) | collective-permute-done | bytes 393248 | tf_op jit(solution)/shard_map/cond/branch_2_fun/ppermute | solution.py:266
  96.3 2.3 pad_maximum_fusion.2
  98.6 3.1 %collective-permute-start.54 = (bf16[2,2,2,4,256,256]{5,4,3,2,1,0:T(8,128)(2,1)}, bf16[2,2,2,4,256,256]{5,4,3,2,1,0:T(8,128)(2,1)}, u32[]{:S(2)}, u32[]{:S(2)}) collective-permute-start(bf16[2,2,2,4,256,256]{5,4,3,2,1,0:T(8,128)(2,1)} %bitcast.20.refs_5_), channel_id=1, source_target_pairs={{0,1},{1,0},{2,3},{3,2},{4,5},{5,4},{6,7},{7,6},{8,9},{9,8},{10,11... | collective-permute-start | bytes 12582920 | tf_op jit(solution)/shard_map/cond/branch_2_fun/ppermute | solution.py:266
  101.7 2.7 %collective-permute-start.52 = (bf16[8,256,256]{2,1,0:T(8,128)(2,1)S(1)}, bf16[8,256,256]{2,1,0:T(8,128)(2,1)}, u32[]{:S(2)}, u32[]{:S(2)}) collective-permute-start(bf16[8,256,256]{2,1,0:T(8,128)(2,1)S(1)} %collective-permute-done.47.refs_0_), channel_id=1, source_target_pairs={{8,16},{16,8},{9,17},{17,9},{10,18},{18,10},{11,19},{19,11},{12,20... | collective-permute-start | bytes 3145736 | tf_op jit(solution)/shard_map/cond/branch_2_fun/ppermute | solution.py:259
  104.4 4.5 %collective-permute-start.53 = (bf16[8,256,256]{2,1,0:T(8,128)(2,1)}, bf16[8,256,256]{2,1,0:T(8,128)(2,1)}, u32[]{:S(2)}, u32[]{:S(2)}) collective-permute-start(bf16[8,256,256]{2,1,0:T(8,128)(2,1)} %collective-permute-done.48), channel_id=1, source_target_pairs={{8,0},{16,24},{9,1},{17,25},{10,2},{18,26},{11,3},{19,27},{12,4},{... | collective-permute-start | bytes 3145736 | tf_op jit(solution)/shard_map/cond/branch_2_fun/ppermute | solution.py:262
  109.6 41.3 %collective-permute-done.55.refs_3_ = bf16[4,256,256]{2,1,0:T(8,128)(2,1)} collective-permute-done((bf16[4,256,256]{2,1,0:T(8,128)(2,1)}, bf16[4,256,256]{2,1,0:T(8,128)(2,1)}, u32[]{:S(2)}, u32[]{:S(2)}) %collective-permute-start.55) | collective-permute-done | bytes 524320 | tf_op jit(solution)/shard_map/cond/branch_2_fun/ppermute | solution.py:266
  151.0 2.3 collective-permute-start.56
  153.3 1.3 broadcast_select_fusion.5.refs_1_
  155.6 9.4 %branch_2_fun.5 = bf16[2,2,4,256,256]{4,3,2,1,0:T(8,128)(2,1)} custom-call(s32[80]{0:T(128)S(1)} %get-tuple-element.123.s_ref, bf16[8,256,256]{2,1,0:T(8,128)(2,1)S(1)} %constant_dynamic-update-slice_fusion.8.refs_0_, bf16[8,256,256]{2,1,0:T(8,128)(2,1)S(1)} %broadcast_select_fusion.5.refs_1_, ...), custom_call_target="tpu_custom_call" | custom-call | flops 2863311616 | bytes 14680064 | tf_op jit(solution)/shard_map/cond/branch_2_fun/pallas_call | solution.py:139
  165.1 5.1 %all-to-all-start.4 = ((bf16[4,4,256,256]{3,2,1,0:T(8,128)(2,1)}), bf16[4,4,256,256]{3,2,1,0:T(8,128)(2,1)}, u32[]{:S(2)}, u32[]{:S(2)}) async-start(bf16[4,4,256,256]{3,2,1,0:T(8,128)(2,1)} %bitcast.21), calls=%async_computation.4 | async-start | bytes 4194304 | tf_op jit(solution)/shard_map/cond/branch_2_fun/all_to_all | solution.py:307
  170.2 2.6 %collective-permute-start.57 = (bf16[3,256,256]{2,1,0:T(8,128)(2,1)S(1)}, bf16[3,256,256]{2,1,0:T(8,128)(2,1)S(1)}, u32[]{:S(2)}, u32[]{:S(2)}) collective-permute-start(bf16[3,256,256]{2,1,0:T(8,128)(2,1)S(1)} %copy-done.46), channel_id=1, source_target_pairs={{0,24},{8,16},{16,8},{24,0},{1,25},{9,17},{17,9},{25,1},{2,26},{10... | collective-permute-start | bytes 1179656 | tf_op jit(solution)/shard_map/cond/branch_2_fun/ppermute | solution.py:266
  172.8 10.2 %collective-permute-done.56 = bf16[8,256,256]{2,1,0:T(8,128)(2,1)} collective-permute-done((bf16[8,256,256]{2,1,0:T(8,128)(2,1)}, bf16[8,256,256]{2,1,0:T(8,128)(2,1)}, u32[]{:S(2)}, u32[]{:S(2)}) %collective-permute-start.56) | collective-permute-done | bytes 1048608 | tf_op jit(solution)/shard_map/cond/branch_2_fun/ppermute | solution.py:262
  183.0 1.3 broadcast_select_fusion.4.refs_1_
  184.4 10.6 %branch_2_fun.6 = bf16[2,2,4,256,256]{4,3,2,1,0:T(8,128)(2,1)} custom-call(s32[80]{0:T(128)S(1)} %get-tuple-element.123.s_ref, bf16[8,256,256]{2,1,0:T(8,128)(2,1)S(1)} %collective-permute-done.47.refs_0_, bf16[8,256,256]{2,1,0:T(8,128)(2,1)S(1)} %broadcast_select_fusion.4.refs_1_, bf16[7,256,256]{2,1,0:T(8,128)(2,1)S(1)} %collective-permute-done.45.refs_2_, ...), custom_call_target="tpu_custom_call" | custom-call | flops 2863311616 | bytes 14680064 | tf_op jit(solution)/shard_map/cond/branch_2_fun/pallas_call | solution.py:139
  195.5 6.7 %all-to-all-start.5 = ((bf16[4,4,256,256]{3,2,1,0:T(8,128)(2,1)}), bf16[4,4,256,256]{3,2,1,0:T(8,128)(2,1)S(1)}, u32[]{:S(2)}, u32[]{:S(2)}) async-start(bf16[4,4,256,256]{3,2,1,0:T(8,128)(2,1)} %bitcast.22), calls=%async_computation.5 | async-start | bytes 4194304 | tf_op jit(solution)/shard_map/cond/branch_2_fun/all_to_all | solution.py:307
  202.6 24.2 %all-to-all-done.5.refs_1_ = bf16[4,4,256,256]{3,2,1,0:T(8,128)(2,1)S(1)} async-done(((bf16[4,4,256,256]{3,2,1,0:T(8,128)(2,1)}), bf16[4,4,256,256]{3,2,1,0:T(8,128)(2,1)S(1)}, u32[]{:S(2)}, u32[]{:S(2)}) %all-to-all-start.5) | async-done | bytes 2097184 | tf_op jit(solution)/shard_map/cond/branch_2_fun/all_to_all | solution.py:307
  228.0 3.9 %collective-permute-done.59.refs_3_ = bf16[4,4,256,256]{3,2,1,0:T(8,128)(2,1)} collective-permute-done((bf16[4,4,256,256]{3,2,1,0:T(8,128)(2,1)S(1)}, bf16[4,4,256,256]{3,2,1,0:T(8,128)(2,1)}, u32[]{:S(2)}, u32[]{:S(2)}) %collective-permute-start.59) | collective-permute-done | bytes 2097184 | tf_op jit(solution)/shard_map/cond/branch_2_fun/ppermute | solution.py:266
  231.9 5.6 %branch_2_fun.7 = bf16[4,2,4,256,256]{4,3,2,1,0:T(8,128)(2,1)} custom-call(s32[4]{0:T(128)S(1)} %copy-done.41, bf16[4,4,256,256]{3,2,1,0:T(8,128)(2,1)} %all-to-all-done.4.refs_0_, bf16[4,4,256,256]{3,2,1,0:T(8,128)(2,1)} %copy-done.18, bf16[4,4,256,256]{3,2,1,0:T(8,128)(2,1)} %collective-permute-done.58.refs_2_, ...), custom_call_target="tpu_custom_call" | custom-call | tf_op jit(solution)/shard_map/cond/branch_2_fun/pallas_call | solution.py:171
  (101 shorter events, 20.2 us)
Async XLA Ops:
  10.1 43.5 %collective-permute-start.44 = (bf16[2,4,256,256]{3,2,1,0:T(8,128)(2,1)}, bf16[2,4,256,256]{3,2,1,0:T(8,128)(2,1)S(1)}, u32[]{:S(2)}, u32[]{:S(2)}) collective-permute-start(bf16[2,4,256,256]{3,2,1,0:T(8,128)(2,1)} %get-tuple-element.229), channel_id=1, source_target_pairs={{0,4},{4,0},{1,5},{5,1},{2,6},{6,2},{3,7},{7,3},{8,12},{12,8},{9,1... | collective-permute-start | bytes 3145736 | tf_op jit(solution)/shard_map/cond/branch_2_fun/ppermute | solution.py:266
  11.3 42.3 %collective-permute-start.43 = (bf16[2,4,256,256]{3,2,1,0:T(8,128)(2,1)}, bf16[2,4,256,256]{3,2,1,0:T(8,128)(2,1)S(1)}, u32[]{:S(2)}, u32[]{:S(2)}) collective-permute-start(bf16[2,4,256,256]{3,2,1,0:T(8,128)(2,1)} %get-tuple-element.229), channel_id=1, source_target_pairs={{0,2},{2,0},{1,3},{3,1},{4,6},{6,4},{5,7},{7,5},{8,10},{10,8},{9,1... | collective-permute-start | bytes 3145736 | tf_op jit(solution)/shard_map/cond/branch_2_fun/ppermute | solution.py:266
  20.9 40.9 %copy-start.48 = (bf16[3,256,256]{2,1,0:T(8,128)(2,1)S(1)}, bf16[3,256,256]{2,1,0:T(8,128)(2,1)}, u32[]{:S(2)}) copy-start(bf16[3,256,256]{2,1,0:T(8,128)(2,1)} %get-tuple-element.140) | copy-start | bytes 1179652 | tf_op jit(solution)/shard_map/cond
  20.9 75.4 %copy-start.14 = (bf16[2,4,256,256]{3,2,1,0:T(8,128)(2,1)S(1)}, bf16[2,4,256,256]{3,2,1,0:T(8,128)(2,1)}, u32[]{:S(2)}) copy-start(bf16[2,4,256,256]{3,2,1,0:T(8,128)(2,1)} %get-tuple-element.229) | copy-start | bytes 3145732 | tf_op jit(solution)/shard_map/cond
  20.9 32.6 %collective-permute-start.45 = (bf16[7,256,256]{2,1,0:T(8,128)(2,1)}, bf16[7,256,256]{2,1,0:T(8,128)(2,1)S(1)}, u32[]{:S(2)}, u32[]{:S(2)}) collective-permute-start(bf16[7,256,256]{2,1,0:T(8,128)(2,1)} %get-tuple-element.132), channel_id=1, source_target_pairs={{0,8},{8,0},{16,24},{24,16},{1,9},{9,1},{17,25},{25,17},{2,10},{10... | collective-permute-start | bytes 2752520 | tf_op jit(solution)/shard_map/cond/branch_2_fun/ppermute | solution.py:266
  21.5 3.0 %collective-permute-start.40 = (bf16[2,256,256]{2,1,0:T(8,128)(2,1)}, bf16[2,256,256]{2,1,0:T(8,128)(2,1)S(1)}, u32[]{:S(2)}, u32[]{:S(2)}) collective-permute-start(bf16[2,256,256]{2,1,0:T(8,128)(2,1)} %get-tuple-element.128), channel_id=1, source_target_pairs={{0,1},{1,0},{2,3},{3,2},{4,5},{5,4},{6,7},{7,6},{8,9},{9,8},{10,11... | collective-permute-start | bytes 786440 | tf_op jit(solution)/shard_map/cond/branch_2_fun/ppermute | solution.py:270
  23.1 17.7 %collective-permute-start.41 = (bf16[2,256,256]{2,1,0:T(8,128)(2,1)}, bf16[2,256,256]{2,1,0:T(8,128)(2,1)S(1)}, u32[]{:S(2)}, u32[]{:S(2)}) collective-permute-start(bf16[2,256,256]{2,1,0:T(8,128)(2,1)} %get-tuple-element.129), channel_id=1, source_target_pairs={{0,2},{1,3},{2,0},{3,1},{4,6},{5,7},{6,4},{7,5},{8,10},{9,11},{10,... | collective-permute-start | bytes 786440 | tf_op jit(solution)/shard_map/cond/branch_2_fun/ppermute | solution.py:270
  24.5 29.1 %collective-permute-start.46 = (bf16[4,256,256]{2,1,0:T(8,128)(2,1)}, bf16[4,256,256]{2,1,0:T(8,128)(2,1)S(1)}, u32[]{:S(2)}, u32[]{:S(2)}) collective-permute-start(bf16[4,256,256]{2,1,0:T(8,128)(2,1)} %get-tuple-element.133), channel_id=1, source_target_pairs={{0,16},{8,24},{16,0},{24,8},{1,17},{9,25},{17,1},{25,9},{2,18},{10... | collective-permute-start | bytes 1572872 | tf_op jit(solution)/shard_map/cond/branch_2_fun/ppermute | solution.py:266
  40.8 10.3 %collective-permute-start.42 = (bf16[2,256,256]{2,1,0:T(8,128)(2,1)}, bf16[2,256,256]{2,1,0:T(8,128)(2,1)S(1)}, u32[]{:S(2)}, u32[]{:S(2)}) collective-permute-start(bf16[2,256,256]{2,1,0:T(8,128)(2,1)} %get-tuple-element.130), channel_id=1, source_target_pairs={{0,3},{1,2},{2,1},{3,0},{4,7},{5,6},{6,5},{7,4},{8,11},{9,10},{10,... | collective-permute-start | bytes 786440 | tf_op jit(solution)/shard_map/cond/branch_2_fun/ppermute | solution.py:270
  53.6 2.2 copy-start.24
  53.6 1.0 copy-start.32
  54.6 41.7 %copy-start.33 = (bf16[2,4,256,256]{3,2,1,0:T(8,128)(2,1)S(1)}, bf16[2,4,256,256]{3,2,1,0:T(8,128)(2,1)}, u32[]{:S(2)}) copy-start(bf16[2,4,256,256]{3,2,1,0:T(8,128)(2,1)} %copy-done.32) | copy-start | bytes 3145732 | tf_op jit(solution)/shard_map/cond
  55.7 40.4 %collective-permute-start.48 = (bf16[8,256,256]{2,1,0:T(8,128)(2,1)S(1)}, bf16[8,256,256]{2,1,0:T(8,128)(2,1)}, u32[]{:S(2)}, u32[]{:S(2)}) collective-permute-start(bf16[8,256,256]{2,1,0:T(8,128)(2,1)S(1)} %constant_dynamic-update-slice_fusion.8.refs_0_), channel_id=1, source_target_pairs={{8,16},{16,8},{9,17},{17,9},{10,18},{18,10},{11,19},{19,11},{12,20... | collective-permute-start | bytes 3145736 | tf_op jit(solution)/shard_map/cond/branch_2_fun/ppermute | solution.py:259
  58.3 38.0 %copy-start.25 = (bf16[2,4,256,256]{3,2,1,0:T(8,128)(2,1)S(1)}, bf16[2,4,256,256]{3,2,1,0:T(8,128)(2,1)}, u32[]{:S(2)}) copy-start(bf16[2,4,256,256]{3,2,1,0:T(8,128)(2,1)} %copy-done.24) | copy-start | bytes 3145732 | tf_op jit(solution)/shard_map/cond
  58.3 37.9 %collective-permute-start.47 = (bf16[8,256,256]{2,1,0:T(8,128)(2,1)S(1)}, bf16[8,256,256]{2,1,0:T(8,128)(2,1)S(1)}, u32[]{:S(2)}, u32[]{:S(2)}) collective-permute-start(bf16[8,256,256]{2,1,0:T(8,128)(2,1)S(1)} %constant_dynamic-update-slice_fusion.8.refs_0_), channel_id=1, source_target_pairs={{0,8},{8,0},{16,24},{24,16},{1,9},{9,1},{17,25},{25,17},{2,10},{10... | collective-permute-start | bytes 3145736 | tf_op jit(solution)/shard_map/cond/branch_2_fun/ppermute | solution.py:266
  60.6 35.5 %collective-permute-start.50 = (bf16[1,4,256,256]{3,2,1,0:T(8,128)(2,1)S(1)}, bf16[1,4,256,256]{3,2,1,0:T(8,128)(2,1)S(1)}, u32[]{:S(2)}, u32[]{:S(2)}) collective-permute-start(bf16[1,4,256,256]{3,2,1,0:T(8,128)(2,1)S(1)} %slice.30), channel_id=1, source_target_pairs={{0,2},{2,0},{1,3},{3,1},{4,6},{6,4},{5,7},{7,5},{8,10},{10,8},{9,1... | collective-permute-start | bytes 1572872 | tf_op jit(solution)/shard_map/cond/branch_2_fun/ppermute | solution.py:266
  61.3 34.9 %collective-permute-start.49 = (bf16[1,4,256,256]{3,2,1,0:T(8,128)(2,1)S(1)}, bf16[1,4,256,256]{3,2,1,0:T(8,128)(2,1)S(1)}, u32[]{:S(2)}, u32[]{:S(2)}) collective-permute-start(bf16[1,4,256,256]{3,2,1,0:T(8,128)(2,1)S(1)} %slice.29), channel_id=1, source_target_pairs={{0,4},{4,0},{1,5},{5,1},{2,6},{6,2},{3,7},{7,3},{8,12},{12,8},{9,1... | collective-permute-start | bytes 1572872 | tf_op jit(solution)/shard_map/cond/branch_2_fun/ppermute | solution.py:266
  61.7 33.7 %collective-permute-start.51 = (bf16[3,256,256]{2,1,0:T(8,128)(2,1)S(1)}, bf16[3,256,256]{2,1,0:T(8,128)(2,1)S(1)}, u32[]{:S(2)}, u32[]{:S(2)}) collective-permute-start(bf16[3,256,256]{2,1,0:T(8,128)(2,1)S(1)} %copy-done.48), channel_id=1, source_target_pairs={{0,16},{8,24},{16,0},{24,8},{1,17},{9,25},{17,1},{25,9},{2,18},{10... | collective-permute-start | bytes 1179656 | tf_op jit(solution)/shard_map/cond/branch_2_fun/ppermute | solution.py:266
  98.6 52.3 %collective-permute-start.54 = (bf16[2,2,2,4,256,256]{5,4,3,2,1,0:T(8,128)(2,1)}, bf16[2,2,2,4,256,256]{5,4,3,2,1,0:T(8,128)(2,1)}, u32[]{:S(2)}, u32[]{:S(2)}) collective-permute-start(bf16[2,2,2,4,256,256]{5,4,3,2,1,0:T(8,128)(2,1)} %bitcast.20.refs_5_), channel_id=1, source_target_pairs={{0,1},{1,0},{2,3},{3,2},{4,5},{5,4},{6,7},{7,6},{8,9},{9,8},{10,11... | collective-permute-start | bytes 12582920 | tf_op jit(solution)/shard_map/cond/branch_2_fun/ppermute | solution.py:266
  101.7 49.3 %collective-permute-start.52 = (bf16[8,256,256]{2,1,0:T(8,128)(2,1)S(1)}, bf16[8,256,256]{2,1,0:T(8,128)(2,1)}, u32[]{:S(2)}, u32[]{:S(2)}) collective-permute-start(bf16[8,256,256]{2,1,0:T(8,128)(2,1)S(1)} %collective-permute-done.47.refs_0_), channel_id=1, source_target_pairs={{8,16},{16,8},{9,17},{17,9},{10,18},{18,10},{11,19},{19,11},{12,20... | collective-permute-start | bytes 3145736 | tf_op jit(solution)/shard_map/cond/branch_2_fun/ppermute | solution.py:259
  104.4 46.5 %collective-permute-start.53 = (bf16[8,256,256]{2,1,0:T(8,128)(2,1)}, bf16[8,256,256]{2,1,0:T(8,128)(2,1)}, u32[]{:S(2)}, u32[]{:S(2)}) collective-permute-start(bf16[8,256,256]{2,1,0:T(8,128)(2,1)} %collective-permute-done.48), channel_id=1, source_target_pairs={{8,0},{16,24},{9,1},{17,25},{10,2},{18,26},{11,3},{19,27},{12,4},{... | collective-permute-start | bytes 3145736 | tf_op jit(solution)/shard_map/cond/branch_2_fun/ppermute | solution.py:262
  108.9 42.0 %collective-permute-start.55 = (bf16[4,256,256]{2,1,0:T(8,128)(2,1)}, bf16[4,256,256]{2,1,0:T(8,128)(2,1)}, u32[]{:S(2)}, u32[]{:S(2)}) collective-permute-start(bf16[4,256,256]{2,1,0:T(8,128)(2,1)} %get-tuple-element.145), channel_id=1, source_target_pairs={{0,24},{8,16},{16,8},{24,0},{1,25},{9,17},{17,9},{25,1},{2,26},{10... | collective-permute-start | bytes 1572872 | tf_op jit(solution)/shard_map/cond/branch_2_fun/ppermute | solution.py:266
  151.0 32.0 %collective-permute-start.56 = (bf16[8,256,256]{2,1,0:T(8,128)(2,1)}, bf16[8,256,256]{2,1,0:T(8,128)(2,1)}, u32[]{:S(2)}, u32[]{:S(2)}) collective-permute-start(bf16[8,256,256]{2,1,0:T(8,128)(2,1)} %collective-permute-done.52), channel_id=1, source_target_pairs={{8,0},{16,24},{9,1},{17,25},{10,2},{18,26},{11,3},{19,27},{12,4},{... | collective-permute-start | bytes 3145736 | tf_op jit(solution)/shard_map/cond/branch_2_fun/ppermute | solution.py:262
  154.6 1.0 copy-start.9
  165.1 5.1 %copy-start.46 = (bf16[3,256,256]{2,1,0:T(8,128)(2,1)S(1)}, bf16[3,256,256]{2,1,0:T(8,128)(2,1)}, u32[]{:S(2)}) copy-start(bf16[3,256,256]{2,1,0:T(8,128)(2,1)} %get-tuple-element.153) | copy-start | bytes 1179652 | tf_op jit(solution)/shard_map/cond
  165.1 30.4 %all-to-all-start.4 = ((bf16[4,4,256,256]{3,2,1,0:T(8,128)(2,1)}), bf16[4,4,256,256]{3,2,1,0:T(8,128)(2,1)}, u32[]{:S(2)}, u32[]{:S(2)}) async-start(bf16[4,4,256,256]{3,2,1,0:T(8,128)(2,1)} %bitcast.21), calls=%async_computation.4 | async-start | bytes 4194304 | tf_op jit(solution)/shard_map/cond/branch_2_fun/all_to_all | solution.py:307
  170.2 14.2 %collective-permute-start.57 = (bf16[3,256,256]{2,1,0:T(8,128)(2,1)S(1)}, bf16[3,256,256]{2,1,0:T(8,128)(2,1)S(1)}, u32[]{:S(2)}, u32[]{:S(2)}) collective-permute-start(bf16[3,256,256]{2,1,0:T(8,128)(2,1)S(1)} %copy-done.46), channel_id=1, source_target_pairs={{0,24},{8,16},{16,8},{24,0},{1,25},{9,17},{17,9},{25,1},{2,26},{10... | collective-permute-start | bytes 1179656 | tf_op jit(solution)/shard_map/cond/branch_2_fun/ppermute | solution.py:266
  194.9 37.0 %copy-start.41 = (s32[4]{0:T(128)S(1)}, s32[4]{0:T(128)}, u32[]{:S(2)}) copy-start(s32[4]{0:T(128)} %copy-done.40) | copy-start | bytes 52 | tf_op jit(solution)/shard_map/cond
  195.5 31.3 %all-to-all-start.5 = ((bf16[4,4,256,256]{3,2,1,0:T(8,128)(2,1)}), bf16[4,4,256,256]{3,2,1,0:T(8,128)(2,1)S(1)}, u32[]{:S(2)}, u32[]{:S(2)}) async-start(bf16[4,4,256,256]{3,2,1,0:T(8,128)(2,1)} %bitcast.22), calls=%async_computation.5 | async-start | bytes 4194304 | tf_op jit(solution)/shard_map/cond/branch_2_fun/all_to_all | solution.py:307
  202.2 25.8 %collective-permute-start.58 = (bf16[4,4,256,256]{3,2,1,0:T(8,128)(2,1)}, bf16[4,4,256,256]{3,2,1,0:T(8,128)(2,1)}, u32[]{:S(2)}, u32[]{:S(2)}) collective-permute-start(bf16[4,4,256,256]{3,2,1,0:T(8,128)(2,1)} %all-to-all-done.4.refs_0_), channel_id=1, source_target_pairs={{0,1},{1,0},{2,3},{3,2},{4,5},{5,4},{6,7},{7,6},{8,9},{9,8},{10,11... | collective-permute-start | bytes 6291464 | tf_op jit(solution)/shard_map/cond/branch_2_fun/ppermute | solution.py:266
  226.8 5.1 %copy-start.18 = (bf16[4,4,256,256]{3,2,1,0:T(8,128)(2,1)}, bf16[4,4,256,256]{3,2,1,0:T(8,128)(2,1)S(1)}, u32[]{:S(2)}) copy-start(bf16[4,4,256,256]{3,2,1,0:T(8,128)(2,1)S(1)} %all-to-all-done.5.refs_1_) | copy-start | bytes 6291460 | tf_op jit(solution)/shard_map/cond
  226.8 5.1 %collective-permute-start.59 = (bf16[4,4,256,256]{3,2,1,0:T(8,128)(2,1)S(1)}, bf16[4,4,256,256]{3,2,1,0:T(8,128)(2,1)}, u32[]{:S(2)}, u32[]{:S(2)}) collective-permute-start(bf16[4,4,256,256]{3,2,1,0:T(8,128)(2,1)S(1)} %all-to-all-done.5.refs_1_), channel_id=1, source_target_pairs={{0,1},{1,0},{2,3},{3,2},{4,5},{5,4},{6,7},{7,6},{8,9},{9,8},{10,11... | collective-permute-start | bytes 6291464 | tf_op jit(solution)/shard_map/cond/branch_2_fun/ppermute | solution.py:266
  (5 other events, 3.1 us)

commit v3 on v2

--- a/solution.py
+++ b/solution.py
@@ -45,76 +45,76 @@
 
 
 def block_kernel(
-    group, planes, cols, terms, pieces, slots_at, s_ref, l_refs, p_refs, r_refs, out_ref
+    d, planes, cols, terms, pieces, slots_at, s_ref, l_ref, p_refs, r_refs, out_ref
 ):
     f = pl.program_id(0)
     i = pl.program_id(1)
-    z = s_ref[0]
     sizes_at = HEAD + planes * 2 * cols
     nr = s_ref[sizes_at + planes + f * cols + i]
     width = out_ref.shape[-1]
     per = terms // planes
-    for at, d in enumerate(group):
-        link = s_ref[HEAD + (d * 2 + f) * cols + i]
-        nq = s_ref[sizes_at + d]
-        slot = (z ^ d) // 2
-
-        @pl.when(link > 0)
-        def _(at=at, d=d, nq=nq, slot=slot):
-            rows = lax.broadcasted_iota(jnp.int32, (width, width), 0)
-            lanes = lax.broadcasted_iota(jnp.int32, (width, width), 1)
-            keep = (rows < nq) & (lanes < nr)
-            if pieces[d] == [None]:
-                psi = p_refs[at][0][0, 0]
-            else:
-                psi = p_refs[at][0][0]
-                for (_, first, _), ref in zip(pieces[d][1:], p_refs[at][1:]):
-                    held = s_ref[slots_at + (d * 2 + f) * cols + i] >= first
-                    psi = jnp.where(held, ref[0], psi)
-            psi = jnp.where(keep, psi.astype(jnp.float32), 0.0).astype(jnp.bfloat16)
-            total = jnp.zeros((width, width), jnp.float32)
-            for e in range(planes):
-                for kk in range(per):
-                    left = l_refs[at][e * per + kk]
-                    upper = jnp.dot(left, psi, preferred_element_type=jnp.float32)
-                    total += lax.dot_general(
-                        upper.astype(jnp.bfloat16),
-                        r_refs[e % 2][0, e // 2, kk, 0],
-                        (((1,), (1,)), ((), ())),
-                        preferred_element_type=jnp.float32,
-                    )
-            out_ref[0, slot, 0] = jnp.where(keep, total, 0.0).astype(out_ref.dtype)
-
-        @pl.when(link == 0)
-        def _(slot=slot):
-            out_ref[0, slot, 0] = jnp.zeros((width, width), out_ref.dtype)
-
-
-def multiply(group, room, scalars, lefts, psis, rights):
-    terms, width = lefts[0].shape[0], lefts[0].shape[-1]
+    link = s_ref[HEAD + (d * 2 + f) * cols + i]
+    nq = s_ref[sizes_at + d]
+
+    @pl.when(link > 0)
+    def _():
+        rows = lax.broadcasted_iota(jnp.int32, (width, width), 0)
+        lanes = lax.broadcasted_iota(jnp.int32, (width, width), 1)
+        keep = (rows < nq) & (lanes < nr)
+        if d == 0:
+            psi = p_refs[0][0, 0]
+        else:
+            psi = p_refs[0][0]
+            for (_, first, _), ref in zip(pieces[1:], p_refs[1:]):
+                held = s_ref[slots_at + (d * 2 + f) * cols + i] >= first
+                psi = jnp.where(held, ref[0], psi)
+        psi = jnp.where(keep, psi.astype(jnp.float32), 0.0).astype(jnp.bfloat16)
+        total = jnp.zeros((width, width), jnp.float32)
+        for e in range(planes):
+            for kk in range(per):
+                left = l_ref[e * per + kk]
+                upper = jnp.dot(left, psi, preferred_element_type=jnp.float32)
+                total += lax.dot_general(
+                    upper.astype(jnp.bfloat16),
+                    r_refs[e % 2][0, e // 2, kk, 0],
+                    (((1,), (1,)), ((), ())),
+                    preferred_element_type=jnp.float32,
+                )
+        out_ref[0, 0, 0] = jnp.where(keep, total, 0.0).astype(out_ref.dtype)
+
+    @pl.when(link == 0)
+    def _():
+        out_ref[0, 0, 0] = jnp.zeros((width, width), out_ref.dtype)
+
+
+def multiply(d, room, scalars, left, psis, rights, beside=None):
+    terms, width = left.shape[0], left.shape[-1]
     cols = rights[0].shape[3]
     per = rights[0].shape[2]
-    many = len(group)
     planes = terms // per
-
     slots_at = HEAD + planes * 2 * cols + planes + 2 * cols
-    pieces = {d: [piece for piece in ranges(room) if piece[0] == d] or [None] for d in group}
+    pieces = [piece for piece in ranges(room) if piece[0] == d] or [None]
+    many = len(pieces)
 
     def body(s_ref, *refs):
-        l_refs, p_refs, at = refs[:many], [], many
-        for d in group:
-            p_refs.append(refs[at : at + len(pieces[d])])
-            at += len(pieces[d])
         block_kernel(
-            group, planes, cols, terms, pieces, slots_at, s_ref, l_refs, p_refs,
-            refs[at:-1], refs[-1],
+            d, planes, cols, terms, pieces, slots_at, s_ref, refs[0], refs[1 : 1 + many],
+            refs[1 + many : 3 + many], refs[-1],
         )
 
-    def psi_spec(d, piece):
+    def held(f, i, s):
+        return s[slots_at + planes * 2 * cols + (d * 2 + f) * cols + i]
+
+    def psi_spec(piece):
         if piece is None:
             return pl.BlockSpec(
                 (1, 1, width, width),
-                lambda f, i, s: (s[2] * 2 + s[3], (s[0] * 2 + (f ^ s[1])) * cols + i, 0, 0),
+                lambda f, i, s: (
+                    s[2] * 2 + s[3],
+                    (s[0] * 2 + (held(f, i, s) // cols ^ s[1])) * cols + held(f, i, s) % cols,
+                    0,
+                    0,
+                ),
             )
         _, first, count = piece
 
@@ -124,29 +124,40 @@
 
         return pl.BlockSpec((1, width, width), index)
 
-    grid_spec = pltpu.PrefetchScalarGridSpec(
-        num_scalar_prefetch=1,
-        grid=(2, cols),
-        in_specs=[pl.BlockSpec((terms, width, width), lambda f, i, s: (0, 0, 0))] * many
-        + [psi_spec(d, piece) for d in group for piece in pieces[d]]
-        + [
-            pl.BlockSpec((1, 2, per, 1, width, width), lambda f, i, s: (f, 0, 0, i, 0, 0))
-        ]
-        * 2,
-        out_specs=pl.BlockSpec((1, 2, 1, width, width), lambda f, i, s: (f ^ s[1], 0, i, 0, 0)),
-    )
-    blocks = many * 2 * cols
+    in_specs = [pl.BlockSpec((terms, width, width), lambda f, i, s: (0, 0, 0))]
+    in_specs += [psi_spec(piece) for piece in pieces]
+    in_specs += [
+        pl.BlockSpec(
+            (1, 2, per, 1, width, width),
+            lambda f, i, s: (held(f, i, s) // cols, 0, 0, held(f, i, s) % cols, 0, 0),
+        )
+    ] * 2
+    inputs = [scalars, left, *psis, *rights]
+    aliases = {}
+    if beside is not None:
+        in_specs.append(pl.BlockSpec(memory_space=pl.ANY))
+        aliases = {len(inputs): 0}
+        inputs.append(beside)
+    blocks = 2 * cols
     return pl.pallas_call(
         body,
-        grid_spec=grid_spec,
+        grid_spec=pltpu.PrefetchScalarGridSpec(
+            num_scalar_prefetch=1,
+            grid=(2, cols),
+            in_specs=in_specs,
+            out_specs=pl.BlockSpec(
+                (1, 1, 1, width, width), lambda f, i, s: (f ^ s[1], (s[0] ^ d) // 2, i, 0, 0)
+            ),
+        ),
         out_shape=jax.ShapeDtypeStruct((2, 2, cols, width, width), jnp.bfloat16),
+        input_output_aliases=aliases,
         compiler_params=pltpu.CompilerParams(vmem_limit_bytes=48 * 2**20),
         cost_estimate=pl.CostEstimate(
-            flops=blocks * terms * 4 * width**3 // 3,
-            bytes_accessed=(many * terms + 2 * cols * terms + 2 * blocks) * width * width * 2,
+            flops=blocks * terms * 16 * width**3,
+            bytes_accessed=(terms + blocks * terms + 2 * blocks) * width * width * 2,
             transcendentals=0,
         ),
-    )(scalars, *lefts, *[piece for psi in psis for piece in psi], *rights)
+    )(*inputs)
 
 
 def put_together(place, own_core, other_core):
@@ -200,14 +211,17 @@
     many = len(pieces)
 
     def body(c_ref, s_ref, *refs):
-        half = len(refs) // 2
+        half = many + planes
         for at in range(many):
             refs[half + at][0] = refs[at][0, 0]
 
         @pl.when(pl.program_id(0) == 0)
         def _():
-            for at in range(many, half):
-                refs[half + at][...] = refs[at][:, 0]
+            kept, to_core, to_chip = refs[half + many :]
+            kept[...] = refs[many][:, 0]
+            to_core[:per] = refs[many + 1][:, 0]
+            to_core[per:] = refs[many + 3][:, 0]
+            to_chip[...] = refs[many + 2][:, 0]
 
     def block_of(d, first, count):
         def index(t, c, s):
@@ -230,13 +244,18 @@
             in_specs=[pl.BlockSpec((1, 1, width, width), block_of(*piece)) for piece in pieces]
             + [pl.BlockSpec((per, 1, width, width), sector_of(e)) for e in range(planes)],
             out_specs=[pl.BlockSpec((1, width, width), place_of(count)) for _, _, count in pieces]
-            + [pl.BlockSpec((per, width, width), lambda t, c, s: (0, 0, 0))] * planes,
+            + [
+                pl.BlockSpec((per * many, width, width), lambda t, c, s: (0, 0, 0))
+                for many in (1, 2, 1)
+            ],
         ),
         out_shape=[
             jax.ShapeDtypeStruct((count, width, width), wavefunction.dtype)
             for _, _, count in pieces
         ]
-        + [jax.ShapeDtypeStruct((per, width, width), left_ops.dtype)] * planes,
+        + [
+            jax.ShapeDtypeStruct((per * many, width, width), left_ops.dtype) for many in (1, 2, 1)
+        ],
     )(cells, place, *([wavefunction] * many), *([left_ops] * planes))
     return outs[:many], outs[many:]
 
@@ -247,10 +266,12 @@
     return jnp.sum(jnp.where(upto, mask[..., None, :], 0), axis=-1)
 
 
-def planned(room, place, cell_table, scalars, wavefunction, left_ops, right_ops):
+def planned(
+    room, place, cell_table, left_sizes, right_sizes, links, wavefunction, left_ops, right_ops
+):
     planes = lax.axis_size("z")
-    z, y, x, c = (lax.axis_index(name) for name in ("z", "y", "x", "c"))
-    owned, sectors = wavefunction.shape[:2]
+    z = lax.axis_index("z")
+    sectors = wavefunction.shape[1]
     width = wavefunction.shape[-1]
     cols = sectors // planes // 2
     after = lax.optimization_barrier
@@ -265,43 +286,50 @@
         size = lax.axis_size(axis)
         return lax.ppermute(value, axis, [(i, i ^ bit) for i in range(size)])
 
-    def on_ops(value, bit):
-        pairs = [(i, i ^ bit) for i in range(planes)]
-        return lax.ppermute(value, ("x", "c"), pairs)
-
+    per = left_ops.shape[0]
+    scalars = kernel_scalars(place, wavefunction.shape[0], left_sizes, right_sizes, links)
     cells = cell_table[:, :room].reshape(-1)
     cuts, sectors_cut = cut_out(cells, place, wavefunction, left_ops, planes, room)
-    mine = [sectors_cut[0]] + [on_ops(sectors_cut[e], e) for e in range(1, planes)]
+    cuts, sectors_cut, right_ops = after((cuts, sectors_cut, right_ops))
+    kept, to_core, to_chip = sectors_cut
+    from_core = flip(to_core, "c", 1)
+    from_chip = flip(jnp.concatenate([to_chip, from_core[per:]], axis=0), "x", 1)
+    mine = [kept, from_core[:per], from_chip]
     psis = {0: [wavefunction]}
-    for (d, _, _), cut in zip(ranges(room), cuts):
+    late = cuts[-1]
+    for (d, _, _), cut in zip(ranges(room)[:-1], cuts):
         psis.setdefault(d, []).append(flip(cut, "z", d))
     r_y = flip(right_ops, "y", 1)
-    r_x = flip(right_ops, "x", 1)
-    mine, r_x, r_y, psis[1], psis[2][0] = after((mine, r_x, r_y, psis[1], psis[2][0]))
-    per = right_ops.shape[0]
-    r_xy1 = flip(r_x[: per // 2], "y", 1)
-    r_xy2 = flip(r_y[per // 2 :], "x", 1)
+    r_x1 = flip(right_ops[: per // 2], "x", 1)
+    rest = right_ops[per // 2 :]
+    mine, rest, r_y, r_x1, psis[1], psis[2][0] = after((mine, rest, r_y, r_x1, psis[1], psis[2][0]))
+    r_x2 = flip(rest, "x", 1)
+    r_xy = flip(r_y, "x", 1)
     own = jnp.concatenate(mine, axis=0)
     beside = flip(own, "z", 1)
     inner1 = inner(own)
-    beside, inner1, r_xy1, r_xy2, psis[2][1] = after((beside, inner1, r_xy1, r_xy2, psis[2][1]))
-    r_xy = jnp.concatenate([r_xy1, r_xy2], axis=0)
+    beside, inner1, r_x2, r_xy, psis[2][1] = after((beside, inner1, r_x2, r_xy, psis[2][1]))
+    r_x = jnp.concatenate([r_x1, r_x2], axis=0)
     near = jnp.stack([right_ops, r_x, r_y, r_xy]).reshape(2, 2, *right_ops.shape)
     other = flip(near, "c", 1)
     inner2 = inner(beside)
     outer1 = outer(inner1)
-    inner2, outer1, other, psis[3][0] = after((inner2, outer1, other, psis[3][0]))
     rights = [near, other]
+    lefts = [own, beside, None, None]
+    firsts = [
+        multiply(first, room, scalars, lefts[first], psis[first], rights) for first, _ in GROUPS
+    ]
+    inner2, outer1, firsts, late, psis[3][0] = after((inner2, outer1, firsts, late, psis[3][0]))
     outer2 = outer(inner2)
+    psis[3].append(flip(late, "z", 3))
 
     inside = (z == 1) | (z == 2)
-    lefts = [own, beside, jnp.where(inside, inner2, outer1), jnp.where(inside, inner1, outer2)]
+    lefts[2] = jnp.where(inside, inner2, outer1)
+    lefts[3] = jnp.where(inside, inner1, outer2)
 
     own_core, other_core = [], []
-    for group in GROUPS:
-        done = multiply(
-            group, room, scalars, [lefts[d] for d in group], [psis[d] for d in group], rights
-        )
+    for (_, second), done in zip(GROUPS, firsts):
+        done = multiply(second, room, scalars, lefts[second], psis[second], rights, done)
         done = done.reshape(4, cols, width, width)
         own_core.append(
             lax.all_to_all(done, ("y", "x"), split_axis=0, concat_axis=0, tiled=True)
@@ -310,12 +338,11 @@
     return put_together(place, own_core, other_core)
 
 
-def tables(wavefunction, left_sizes, right_sizes, links):
+def tables(wavefunction, links):
     planes = lax.axis_size("z")
     z, y, x, c = (lax.axis_index(name) for name in ("z", "y", "x", "c"))
     owned, sectors = wavefunction.shape[:2]
     plane_cols = sectors // planes
-    cols = plane_cols // 2
     o = x * 2 + c
     place = jnp.stack([z, y, x, c]).astype(jnp.int32)
     flips = jnp.arange(planes)
@@ -330,26 +357,41 @@
     sector = (z ^ flips)[:, None] * plane_cols + jnp.arange(plane_cols)[None, :]
     cell_table = jnp.sum(jnp.where(hit, sector[:, None, :], 0), axis=-1).astype(jnp.int32)
 
-    q_of = ((z ^ flips) * 2 + y) * owned + o
+    return most, place, cell_table
+
+
+def kernel_scalars(place, owned, left_sizes, right_sizes, links):
+    planes = lax.axis_size("z")
+    z, y, x, c = (lax.axis_index(name) for name in ("z", "y", "x", "c"))
+    plane_cols = links.shape[1] // planes
+    cols = plane_cols // 2
+    marks = (links != 0).astype(jnp.int32)
+
+    q_of = ((z ^ jnp.arange(planes)) * 2 + y) * owned + x * 2 + c
     come = lax.dynamic_slice_in_dim(marks[q_of], z * plane_cols, plane_cols, 1)
     slots = jnp.maximum(running(come) - 1, 0)
 
     def sided(table):
         table = table.reshape(planes, 2, cols)
-        return jnp.where(y > 0, table[:, ::-1], table).reshape(-1)
-
+        return jnp.where(y > 0, table[:, ::-1], table).reshape(planes, plane_cols)
+
+    flags = sided(come)
+    steps = jnp.arange(plane_cols)
+    upto = (steps[:, None] >= steps[None, :]) & (flags[:, None, :] > 0)
+    last = jnp.max(jnp.where(upto, steps, -1), axis=-1)
+    first = jnp.min(jnp.where(flags > 0, steps, plane_cols - 1), axis=-1)
+    held = jnp.where(last >= 0, last, first[:, None])
     r_of = (z * 2 + (y ^ jnp.arange(2)))[:, None] * cols + jnp.arange(cols)[None, :]
-    scalars = jnp.concatenate(
-        [place, sided(come), left_sizes[q_of], right_sizes[r_of.reshape(-1)], sided(slots)]
-    ).astype(jnp.int32)
-    return most, place, cell_table, scalars
+    parts = [place, flags, left_sizes[q_of], right_sizes[r_of.reshape(-1)], sided(slots), held]
+    return jnp.concatenate([part.reshape(-1) for part in parts]).astype(jnp.int32)
 
 
 ROOMS = (5, 6, 7)
 
 
 def sparse(wavefunction, left_ops, right_ops, left_sizes, right_sizes, links):
-    most, *rest = tables(wavefunction, left_sizes, right_sizes, links)
+    most, *rest = tables(wavefunction, links)
+    rest += [left_sizes, right_sizes, links]
     whole = wavefunction.shape[1] // lax.axis_size("z")
     rooms = [room for room in ROOMS if room < whole] + [whole]
     forms = [functools.partial(planned, room) for room in rooms]

time: 236 us -> 222 us (0.941)
  waiting for transfers between devices: 137 us -> 121 us
  Pallas kernels: 32.3 us -> 38.9 us
  local copies, waits for them, and re-layouts: 12.2 us -> 6.4 us
    ppermute x3 -> x0, waiting for transfers between devices: 22.7 us -> none  [on_ops(): return lax.ppermute(value, ('x', 'c'), pairs)]
    ppermute x13 -> x15, waiting for transfers between devices: 78.8 us -> 59.1 us  [flip(): return lax.ppermute(value, axis, [(i, i ^ bit) for i in range(size)])]
    ppermute x2, waiting for transfers between devices: 0.01 us -> 17.8 us  [inner(): return lax.ppermute(value, 'z', [(1, 2), (2, 1)])]
    all_to_all x2, waiting for transfers between devices: 24.8 us -> 36.8 us  [planned(): lax.all_to_all(done, ('y', 'x'), split_axis=0, concat_axis=0, tiled=True)]
    ppermute x13 -> x15, starting transfers between devices: 17.1 us -> 25.5 us  [flip(): return lax.ppermute(value, axis, [(i, i ^ bit) for i in range(size)])]
    pallas_call x2 -> x4, Pallas kernels: 20 us -> 27 us  [multiply(): pl.pallas_call(body, grid_spec=pltpu.PrefetchScalarGridSpec(num_scalar_pr...]
    ppermute x3 -> x0, starting transfers between devices: 4.58 us -> none  [on_ops(): return lax.ppermute(value, ('x', 'c'), pairs)]
    ppermute x2, waiting for transfers between devices: 10.2 us -> 6.76 us  [outer(): return lax.ppermute(value, 'z', [(1, 0), (2, 3)])]
  transfers between devices with their start and end apart: 22 -> 21, of which waited for: 10 -> 7; matrix products, arithmetic and copies ran while one was open for 3% -> 3% of each run, Pallas kernels for 11% -> 12%
where the time goes in v3:
time: 222 us; the launch traced here: 223 us
  waiting for transfers between devices  121 us (55%)
  starting transfers between devices  46.5 us (21%)
  Pallas kernels  38.9 us (18%)
  other arithmetic  9.79 us (4%)
  local copies, waits for them, and re-layouts  6.4 us (3%)
    ppermute x15, waiting for transfers between devices, flip(): return lax.ppermute(value, axis, [(i, i ^ bit) for i in range(size)])  59.1 us
    all_to_all x2, waiting for transfers between devices, planned(): lax.all_to_all(done, ('y', 'x'), split_axis=0, concat_axis=0, tiled=True)  36.8 us
    pallas_call x4, Pallas kernels, multiply(): pl.pallas_call(body, grid_spec=pltpu.PrefetchScalarGridSpec(num_scalar_pr...  27 us
    ppermute x15, starting transfers between devices, flip(): return lax.ppermute(value, axis, [(i, i ^ bit) for i in range(size)])  25.5 us
    ppermute x2, waiting for transfers between devices, inner(): return lax.ppermute(value, 'z', [(1, 2), (2, 1)])  17.8 us
    all_to_all x2, starting transfers between devices, planned(): lax.all_to_all(done, ('y', 'x'), split_axis=0, concat_axis=0, tiled=True)  10.3 us
    ppermute x2, waiting for transfers between devices, outer(): return lax.ppermute(value, 'z', [(1, 0), (2, 3)])  6.76 us
    pallas_call x1, Pallas kernels, cut_out(): pl.pallas_call(body, grid_spec=pltpu.PrefetchScalarGridSpec(num_scalar_pr...  6.24 us
  transfers between devices with their start and end apart: 21, of which 7 were waited for; matrix products, arithmetic and copies ran while one was open for 3% of the time, Pallas kernels for 12%

profile of v3, /device:TPU:9, one launch (start us, length us, event | category | flops | bytes accessed | tf_op | source)
XLA Modules:
  0.0 223.0 jit_solution(16186203288427090516)
XLA Ops:
  2.9 1.9 fusion.8
  5.4 217.6 %conditional.1 = (bf16[8,4,256,256]{3,2,1,0:T(8,128)(2,1)}) conditional(s32[]{:T(128)} %clamp.3, (s32[32,32]{1,0:T(8,128)}, s32[32]{0:T(128)}, s32[32]{0:T(128)}, s32[4]{0:T(128)S(1)}, s32[8,8]{1,0:T(8,128)S(1)}, /*index=5*/bf16[4,32,256,256]{3,2,1,0:T(8,128)(2,1)}, bf16[2,4,256,256]{3,2,1,0:T(8,128)(2,1)}, ...), branch_computations={%region_5.9_spmd, %region_9.13_spmd, %region_13.17_spmd, %region_1... | conditional | flops 68727611392 | bytes 202422656 | solution.py:399
  6.6 6.2 %branch_1_fun.6 = (bf16[6,256,256]{2,1,0:T(8,128)(2,1)}, bf16[3,256,256]{2,1,0:T(8,128)(2,1)}, bf16[3,256,256]{2,1,0:T(8,128)(2,1)}, bf16[3,256,256]{2,1,0:T(8,1...) custom-call(s32[24]{0:T(128)} %reshape.561.c_ref, ...), custom_call_target="tpu_custom_call" | custom-call | tf_op jit(solution)/shard_map/cond/branch_1_fun/pallas_call | solution.py:239
  13.6 1.4 collective-permute-start.21
  15.1 1.3 collective-permute-start.22
  17.7 2.8 %collective-permute-start.24 = (bf16[3,256,256]{2,1,0:T(8,128)(2,1)S(1)}, bf16[3,256,256]{2,1,0:T(8,128)(2,1)S(1)}, u32[]{:S(2)}, u32[]{:S(2)}) collective-permute-start(bf16[3,256,256]{2,1,0:T(8,128)(2,1)S(1)} %copy-done.55), channel_id=1, source_target_pairs={{0,16},{8,24},{16,0},{24,8},{1,17},{9,25},{17,1},{25,9},{2,18},{10... | collective-permute-start | bytes 1179656 | tf_op jit(solution)/shard_map/cond/branch_1_fun/ppermute | solution.py:287
  20.6 21.6 %collective-permute-done.24.refs_1_ = bf16[3,256,256]{2,1,0:T(8,128)(2,1)S(1)} collective-permute-done((bf16[3,256,256]{2,1,0:T(8,128)(2,1)S(1)}, bf16[3,256,256]{2,1,0:T(8,128)(2,1)S(1)}, u32[]{:S(2)}, u32[]{:S(2)}) %collective-permute-start.24) | collective-permute-done | bytes 393248 | tf_op jit(solution)/shard_map/cond/branch_1_fun/ppermute | solution.py:287
  42.3 2.5 %collective-permute-start.26 = (bf16[8,256,256]{2,1,0:T(8,128)(2,1)S(1)}, bf16[8,256,256]{2,1,0:T(8,128)(2,1)S(1)}, u32[]{:S(2)}, u32[]{:S(2)}) collective-permute-start(bf16[8,256,256]{2,1,0:T(8,128)(2,1)S(1)} %constant_dynamic-update-slice_fusion.3.refs_0_), channel_id=1, source_target_pairs={{8,16},{16,8},{9,17},{17,9},{10,18},{18,10},{11,19},{19,11},{12,20... | collective-permute-start | bytes 3145736 | tf_op jit(solution)/shard_map/cond/branch_1_fun/ppermute | solution.py:280
  44.8 1.6 collective-permute-start.28
  46.6 2.5 %collective-permute-start.29 = (bf16[3,256,256]{2,1,0:T(8,128)(2,1)S(1)}, bf16[3,256,256]{2,1,0:T(8,128)(2,1)S(1)}, u32[]{:S(2)}, u32[]{:S(2)}) collective-permute-start(bf16[3,256,256]{2,1,0:T(8,128)(2,1)S(1)} %copy-done.52), channel_id=1, source_target_pairs={{0,16},{8,24},{16,0},{24,8},{1,17},{9,25},{17,1},{25,9},{2,18},{10... | collective-permute-start | bytes 1179656 | tf_op jit(solution)/shard_map/cond/branch_1_fun/ppermute | solution.py:287
  49.1 33.6 %collective-permute-done.29.refs_2_ = bf16[3,256,256]{2,1,0:T(8,128)(2,1)S(1)} collective-permute-done((bf16[3,256,256]{2,1,0:T(8,128)(2,1)S(1)}, bf16[3,256,256]{2,1,0:T(8,128)(2,1)S(1)}, u32[]{:S(2)}, u32[]{:S(2)}) %collective-permute-start.29) | collective-permute-done | bytes 393248 | tf_op jit(solution)/shard_map/cond/branch_1_fun/ppermute | solution.py:287
  84.6 2.3 %pad_maximum_fusion.2 = bf16[4,2,4,256,256]{4,3,2,1,0:T(8,128)(2,1)} fusion(bf16[1,2,4,256,256]{4,3,2,1,0:T(8,128)(2,1)S(1)} %bitcast.78, bf16[1,2,4,256,256]{4,3,2,1,0:T(8,128)(2,1)S(1)} %bitcast.74, bf16[1,2,4,256,256]{4,3,2,1,0:T(8,128)(2,1)S(1)} %maximum_bitcast_fusion.1, bf16[1,2,4,256,256]{4,3,2,1,0:T(8,128)(2,1)S(1)} %bitcast.66), kind=kLoop, calls=%fused_computation.47 | loop fusion | flops 6291456 | bytes 8388608 | tf_op jit(solution)/shard_map/cond/branch_1_fun/stack | solution.py:313
  86.9 2.1 collective-permute-start.32
  89.0 1.1 collective-permute-start.33
  93.6 2.3 %collective-permute-start.30 = (bf16[8,256,256]{2,1,0:T(8,128)(2,1)S(1)}, bf16[8,256,256]{2,1,0:T(8,128)(2,1)}, u32[]{:S(2)}, u32[]{:S(2)}) collective-permute-start(bf16[8,256,256]{2,1,0:T(8,128)(2,1)S(1)} %collective-permute-done.25.refs_0_), channel_id=1, source_target_pairs={{8,16},{16,8},{9,17},{17,9},{10,18},{18,10},{11,19},{19,11},{12,20... | collective-permute-start | bytes 3145736 | tf_op jit(solution)/shard_map/cond/branch_1_fun/ppermute | solution.py:280
  95.9 4.5 %collective-permute-start.31 = (bf16[8,256,256]{2,1,0:T(8,128)(2,1)}, bf16[8,256,256]{2,1,0:T(8,128)(2,1)S(1)}, u32[]{:S(2)}, u32[]{:S(2)}) collective-permute-start(bf16[8,256,256]{2,1,0:T(8,128)(2,1)} %copy-done.31), channel_id=1, source_target_pairs={{8,0},{16,24},{9,1},{17,25},{10,2},{18,26},{11,3},{19,27},{12,4},{... | collective-permute-start | bytes 3145736 | tf_op jit(solution)/shard_map/cond/branch_1_fun/ppermute | solution.py:283
  100.4 4.7 %branch_1_fun.7.refs_5_ = bf16[2,2,4,256,256]{4,3,2,1,0:T(8,128)(2,1)} custom-call(s32[112]{0:T(128)S(1)} %concatenate.36.s_ref, bf16[8,256,256]{2,1,0:T(8,128)(2,1)S(1)} %constant_dynamic-update-slice_fusion.3.refs_0_, bf16[4,32,256,256]{3,2,1,0:T(8,128)(2,1)} %get-tuple-element.300.refs_0_.refs_1_.refs_2_.refs_3_.refs_4_, ...), custom_call_target="tpu_custom_call" | custom-call | flops 17179869184 | bytes 11534336 | tf_op jit(solution)/shard_map/cond/branch_1_fun/pallas_call | solution.py:142
  105.2 8.0 %branch_1_fun.8.refs_5_ = bf16[2,2,4,256,256]{4,3,2,1,0:T(8,128)(2,1)} custom-call(s32[112]{0:T(128)S(1)} %concatenate.36.s_ref, bf16[8,256,256]{2,1,0:T(8,128)(2,1)S(1)} %collective-permute-done.25.refs_0_, bf16[6,256,256]{2,1,0:T(8,128)(2,1)S(1)} %collective-permute-done.23.refs_1_, bf16[2,2,2,4,256,256]{5,4,3,2,1,0:T(8,128)(2,1)} %bitcast.18.refs_2_.refs_3_, ...), custom_call_target="tpu_custom_call" | custom-call | flops 17179869184 | bytes 11534336 | tf_op jit(solution)/shard_map/cond/branch_1_fun/pallas_call | solution.py:142
  113.2 17.8 %collective-permute-done.30 = bf16[8,256,256]{2,1,0:T(8,128)(2,1)} collective-permute-done((bf16[8,256,256]{2,1,0:T(8,128)(2,1)S(1)}, bf16[8,256,256]{2,1,0:T(8,128)(2,1)}, u32[]{:S(2)}, u32[]{:S(2)}) %collective-permute-start.30) | collective-permute-done | bytes 1048608 | tf_op jit(solution)/shard_map/cond/branch_1_fun/ppermute | solution.py:280
  131.0 9.5 %collective-permute-start.35 = (bf16[3,256,256]{2,1,0:T(8,128)(2,1)}, bf16[3,256,256]{2,1,0:T(8,128)(2,1)S(1)}, u32[]{:S(2)}, u32[]{:S(2)}) collective-permute-start(bf16[3,256,256]{2,1,0:T(8,128)(2,1)} %get-tuple-element.160), channel_id=1, source_target_pairs={{0,24},{8,16},{16,8},{24,0},{1,25},{9,17},{17,9},{25,1},{2,26},{10... | collective-permute-start | bytes 1179656 | tf_op jit(solution)/shard_map/cond/branch_1_fun/ppermute | solution.py:287
  140.5 1.3 collective-permute-start.34
  141.9 1.3 broadcast_select_fusion.4.refs_0_
  143.2 7.1 %branch_1_fun.9 = bf16[2,2,4,256,256]{4,3,2,1,0:T(8,128)(2,1)} custom-call(s32[112]{0:T(128)S(1)} %concatenate.36.s_ref, bf16[8,256,256]{2,1,0:T(8,128)(2,1)S(1)} %broadcast_select_fusion.4.refs_0_, bf16[3,256,256]{2,1,0:T(8,128)(2,1)S(1)} %collective-permute-done.24.refs_1_, bf16[3,256,256]{2,1,0:T(8,128)(2,1)S(1)} %copy-done.5, ...), custom_call_target="tpu_custom_call", output_to_operand_aliasing={{}: (6, {})} | custom-call | flops 17179869184 | bytes 11534336 | tf_op jit(solution)/shard_map/cond/branch_1_fun/pallas_call | solution.py:142
  150.3 6.7 %all-to-all-start.2 = ((bf16[4,4,256,256]{3,2,1,0:T(8,128)(2,1)}), bf16[4,4,256,256]{3,2,1,0:T(8,128)(2,1)}, u32[]{:S(2)}, u32[]{:S(2)}) async-start(bf16[4,4,256,256]{3,2,1,0:T(8,128)(2,1)} %bitcast.19), calls=%async_computation.2 | async-start | bytes 4194304 | tf_op jit(solution)/shard_map/cond/branch_1_fun/all_to_all | solution.py:335
  157.0 6.8 %collective-permute-done.34 = bf16[8,256,256]{2,1,0:T(8,128)(2,1)S(1)} collective-permute-done((bf16[8,256,256]{2,1,0:T(8,128)(2,1)}, bf16[8,256,256]{2,1,0:T(8,128)(2,1)S(1)}, u32[]{:S(2)}, u32[]{:S(2)}) %collective-permute-start.34) | collective-permute-done | bytes 1048608 | tf_op jit(solution)/shard_map/cond/branch_1_fun/ppermute | solution.py:283
  163.9 7.2 %branch_1_fun.10 = bf16[2,2,4,256,256]{4,3,2,1,0:T(8,128)(2,1)} custom-call(s32[112]{0:T(128)S(1)} %concatenate.36.s_ref, bf16[8,256,256]{2,1,0:T(8,128)(2,1)S(1)} %broadcast_select_fusion.3.refs_0_, bf16[3,256,256]{2,1,0:T(8,128)(2,1)} %collective-permute-done.33.refs_1_, ...), custom_call_target="tpu_custom_call", output_to_operand_aliasing={{}: (6, {})} | custom-call | flops 17179869184 | bytes 11534336 | tf_op jit(solution)/shard_map/cond/branch_1_fun/pallas_call | solution.py:142
  171.2 12.9 %all-to-all-done.2.refs_0_ = bf16[4,4,256,256]{3,2,1,0:T(8,128)(2,1)} async-done(((bf16[4,4,256,256]{3,2,1,0:T(8,128)(2,1)}), bf16[4,4,256,256]{3,2,1,0:T(8,128)(2,1)}, u32[]{:S(2)}, u32[]{:S(2)}) %all-to-all-start.2) | async-done | bytes 2097184 | tf_op jit(solution)/shard_map/cond/branch_1_fun/all_to_all | solution.py:335
  184.1 3.6 %all-to-all-start.3 = ((bf16[4,4,256,256]{3,2,1,0:T(8,128)(2,1)}), bf16[4,4,256,256]{3,2,1,0:T(8,128)(2,1)S(1)}, u32[]{:S(2)}, u32[]{:S(2)}) async-start(bf16[4,4,256,256]{3,2,1,0:T(8,128)(2,1)} %bitcast.20), calls=%async_computation.3 | async-start | bytes 4194304 | tf_op jit(solution)/shard_map/cond/branch_1_fun/all_to_all | solution.py:335
  188.3 23.8 %all-to-all-done.3.refs_1_ = bf16[4,4,256,256]{3,2,1,0:T(8,128)(2,1)S(1)} async-done(((bf16[4,4,256,256]{3,2,1,0:T(8,128)(2,1)}), bf16[4,4,256,256]{3,2,1,0:T(8,128)(2,1)S(1)}, u32[]{:S(2)}, u32[]{:S(2)}) %all-to-all-start.3) | async-done | bytes 2097184 | tf_op jit(solution)/shard_map/cond/branch_1_fun/all_to_all | solution.py:335
  212.2 1.4 collective-permute-start.37
  213.5 3.9 %collective-permute-done.37.refs_3_ = bf16[4,4,256,256]{3,2,1,0:T(8,128)(2,1)} collective-permute-done((bf16[4,4,256,256]{3,2,1,0:T(8,128)(2,1)S(1)}, bf16[4,4,256,256]{3,2,1,0:T(8,128)(2,1)}, u32[]{:S(2)}, u32[]{:S(2)}) %collective-permute-start.37) | collective-permute-done | bytes 2097184 | tf_op jit(solution)/shard_map/cond/branch_1_fun/ppermute | solution.py:287
  217.4 5.6 %branch_1_fun.11 = bf16[4,2,4,256,256]{4,3,2,1,0:T(8,128)(2,1)} custom-call(s32[4]{0:T(128)S(1)} %copy-done.46, bf16[4,4,256,256]{3,2,1,0:T(8,128)(2,1)} %all-to-all-done.2.refs_0_, bf16[4,4,256,256]{3,2,1,0:T(8,128)(2,1)} %copy-done.27, bf16[4,4,256,256]{3,2,1,0:T(8,128)(2,1)} %collective-permute-done.36.refs_2_, ...), custom_call_target="tpu_custom_call" | custom-call | tf_op jit(solution)/shard_map/cond/branch_1_fun/pallas_call | solution.py:182
  (111 shorter events, 12.4 us)
Async XLA Ops:
  5.5 7.4 %copy-start.45 = (s32[4]{0:T(128)}, s32[4]{0:T(128)S(1)}, u32[]{:S(2)}) copy-start(s32[4]{0:T(128)S(1)} %get-tuple-element.118.s_ref) | copy-start | bytes 52 | tf_op jit(solution)/shard_map/cond
  6.6 7.0 %copy-start.20 = (bf16[2,4,256,256]{3,2,1,0:T(8,128)(2,1)S(1)}, bf16[2,4,256,256]{3,2,1,0:T(8,128)(2,1)}, u32[]{:S(2)}) copy-start(bf16[2,4,256,256]{3,2,1,0:T(8,128)(2,1)} %get-tuple-element.137) | copy-start | bytes 3145732 | tf_op jit(solution)/shard_map/cond
  12.8 29.3 %copy-start.40 = (bf16[2,256,256]{2,1,0:T(8,128)(2,1)S(1)}, bf16[2,256,256]{2,1,0:T(8,128)(2,1)}, u32[]{:S(2)}) copy-start(bf16[2,256,256]{2,1,0:T(8,128)(2,1)} %get-tuple-element.140) | copy-start | bytes 786436 | tf_op jit(solution)/shard_map/cond
  12.8 33.7 %copy-start.52 = (bf16[3,256,256]{2,1,0:T(8,128)(2,1)S(1)}, bf16[3,256,256]{2,1,0:T(8,128)(2,1)}, u32[]{:S(2)}) copy-start(bf16[3,256,256]{2,1,0:T(8,128)(2,1)} %get-tuple-element.145) | copy-start | bytes 1179652 | tf_op jit(solution)/shard_map/cond
  12.9 71.7 %copy-start.21 = (bf16[2,4,256,256]{3,2,1,0:T(8,128)(2,1)S(1)}, bf16[2,4,256,256]{3,2,1,0:T(8,128)(2,1)}, u32[]{:S(2)}) copy-start(bf16[2,4,256,256]{3,2,1,0:T(8,128)(2,1)} %get-tuple-element.137) | copy-start | bytes 3145732 | tf_op jit(solution)/shard_map/cond
  12.9 3.5 %collective-permute-start.19 = (bf16[4,256,256]{2,1,0:T(8,128)(2,1)}, bf16[4,256,256]{2,1,0:T(8,128)(2,1)S(1)}, u32[]{:S(2)}, u32[]{:S(2)}) collective-permute-start(bf16[4,256,256]{2,1,0:T(8,128)(2,1)} %get-tuple-element.135), channel_id=1, source_target_pairs={{0,1},{1,0},{2,3},{3,2},{4,5},{5,4},{6,7},{7,6},{8,9},{9,8},{10,11... | collective-permute-start | bytes 1572872 | tf_op jit(solution)/shard_map/cond/branch_1_fun/ppermute | solution.py:287
  13.6 28.6 %collective-permute-start.23 = (bf16[6,256,256]{2,1,0:T(8,128)(2,1)}, bf16[6,256,256]{2,1,0:T(8,128)(2,1)S(1)}, u32[]{:S(2)}, u32[]{:S(2)}) collective-permute-start(bf16[6,256,256]{2,1,0:T(8,128)(2,1)} %get-tuple-element.138), channel_id=1, source_target_pairs={{0,8},{8,0},{16,24},{24,16},{1,9},{9,1},{17,25},{25,17},{2,10},{10... | collective-permute-start | bytes 2359304 | tf_op jit(solution)/shard_map/cond/branch_1_fun/ppermute | solution.py:287
  13.6 28.6 %collective-permute-start.21 = (bf16[2,4,256,256]{3,2,1,0:T(8,128)(2,1)S(1)}, bf16[2,4,256,256]{3,2,1,0:T(8,128)(2,1)S(1)}, u32[]{:S(2)}, u32[]{:S(2)}) collective-permute-start(bf16[2,4,256,256]{3,2,1,0:T(8,128)(2,1)S(1)} %copy-done.20), channel_id=1, source_target_pairs={{0,4},{4,0},{1,5},{5,1},{2,6},{6,2},{3,7},{7,3},{8,12},{12,8},{9,1... | collective-permute-start | bytes 3145736 | tf_op jit(solution)/shard_map/cond/branch_1_fun/ppermute | solution.py:287
  15.1 27.1 %collective-permute-start.22 = (bf16[1,4,256,256]{3,2,1,0:T(8,128)(2,1)S(1)}, bf16[1,4,256,256]{3,2,1,0:T(8,128)(2,1)S(1)}, u32[]{:S(2)}, u32[]{:S(2)}) collective-permute-start(bf16[1,4,256,256]{3,2,1,0:T(8,128)(2,1)S(1)} %get-tuple-element.463), channel_id=1, source_target_pairs={{0,2},{2,0},{1,3},{3,1},{4,6},{6,4},{5,7},{7,5},{8,10},{10,8},{9,1... | collective-permute-start | bytes 1572872 | tf_op jit(solution)/shard_map/cond/branch_1_fun/ppermute | solution.py:287
  17.4 24.7 %collective-permute-start.20 = (bf16[4,256,256]{2,1,0:T(8,128)(2,1)S(1)}, bf16[4,256,256]{2,1,0:T(8,128)(2,1)S(1)}, u32[]{:S(2)}, u32[]{:S(2)}) collective-permute-start(bf16[4,256,256]{2,1,0:T(8,128)(2,1)S(1)} %pad_maximum_fusion.3), channel_id=1, source_target_pairs={{0,2},{2,0},{1,3},{3,1},{4,6},{6,4},{5,7},{7,5},{8,10},{10,8},{9,1... | collective-permute-start | bytes 1572872 | tf_op jit(solution)/shard_map/cond/branch_1_fun/ppermute | solution.py:287
  17.7 24.4 %collective-permute-start.24 = (bf16[3,256,256]{2,1,0:T(8,128)(2,1)S(1)}, bf16[3,256,256]{2,1,0:T(8,128)(2,1)S(1)}, u32[]{:S(2)}, u32[]{:S(2)}) collective-permute-start(bf16[3,256,256]{2,1,0:T(8,128)(2,1)S(1)} %copy-done.55), channel_id=1, source_target_pairs={{0,16},{8,24},{16,0},{24,8},{1,17},{9,25},{17,1},{25,9},{2,18},{10... | collective-permute-start | bytes 1179656 | tf_op jit(solution)/shard_map/cond/branch_1_fun/ppermute | solution.py:287
  42.3 41.1 %collective-permute-start.26 = (bf16[8,256,256]{2,1,0:T(8,128)(2,1)S(1)}, bf16[8,256,256]{2,1,0:T(8,128)(2,1)S(1)}, u32[]{:S(2)}, u32[]{:S(2)}) collective-permute-start(bf16[8,256,256]{2,1,0:T(8,128)(2,1)S(1)} %constant_dynamic-update-slice_fusion.3.refs_0_), channel_id=1, source_target_pairs={{8,16},{16,8},{9,17},{17,9},{10,18},{18,10},{11,19},{19,11},{12,20... | collective-permute-start | bytes 3145736 | tf_op jit(solution)/shard_map/cond/branch_1_fun/ppermute | solution.py:280
  44.8 38.7 %collective-permute-start.25 = (bf16[8,256,256]{2,1,0:T(8,128)(2,1)S(1)}, bf16[8,256,256]{2,1,0:T(8,128)(2,1)S(1)}, u32[]{:S(2)}, u32[]{:S(2)}) collective-permute-start(bf16[8,256,256]{2,1,0:T(8,128)(2,1)S(1)} %constant_dynamic-update-slice_fusion.3.refs_0_), channel_id=1, source_target_pairs={{0,8},{8,0},{16,24},{24,16},{1,9},{9,1},{17,25},{25,17},{2,10},{10... | collective-permute-start | bytes 3145736 | tf_op jit(solution)/shard_map/cond/branch_1_fun/ppermute | solution.py:287
  44.8 39.6 %collective-permute-start.28 = (bf16[2,4,256,256]{3,2,1,0:T(8,128)(2,1)S(1)}, bf16[2,4,256,256]{3,2,1,0:T(8,128)(2,1)S(1)}, u32[]{:S(2)}, u32[]{:S(2)}) collective-permute-start(bf16[2,4,256,256]{3,2,1,0:T(8,128)(2,1)S(1)} %collective-permute-done.21), channel_id=1, source_target_pairs={{0,2},{2,0},{1,3},{3,1},{4,6},{6,4},{5,7},{7,5},{8,10},{10,8},{9,1... | collective-permute-start | bytes 3145736 | tf_op jit(solution)/shard_map/cond/branch_1_fun/ppermute | solution.py:287
  46.5 37.0 %collective-permute-start.27 = (bf16[1,4,256,256]{3,2,1,0:T(8,128)(2,1)S(1)}, bf16[1,4,256,256]{3,2,1,0:T(8,128)(2,1)S(1)}, u32[]{:S(2)}, u32[]{:S(2)}) collective-permute-start(bf16[1,4,256,256]{3,2,1,0:T(8,128)(2,1)S(1)} %get-tuple-element.143), channel_id=1, source_target_pairs={{0,2},{2,0},{1,3},{3,1},{4,6},{6,4},{5,7},{7,5},{8,10},{10,8},{9,1... | collective-permute-start | bytes 1572872 | tf_op jit(solution)/shard_map/cond/branch_1_fun/ppermute | solution.py:287
  46.6 36.1 %collective-permute-start.29 = (bf16[3,256,256]{2,1,0:T(8,128)(2,1)S(1)}, bf16[3,256,256]{2,1,0:T(8,128)(2,1)S(1)}, u32[]{:S(2)}, u32[]{:S(2)}) collective-permute-start(bf16[3,256,256]{2,1,0:T(8,128)(2,1)S(1)} %copy-done.52), channel_id=1, source_target_pairs={{0,16},{8,24},{16,0},{24,8},{1,17},{9,25},{17,1},{25,9},{2,18},{10... | collective-permute-start | bytes 1179656 | tf_op jit(solution)/shard_map/cond/branch_1_fun/ppermute | solution.py:287
  84.6 5.7 %copy-start.11 = (s32[32]{0:T(128)S(1)}, s32[32]{0:T(128)}, u32[]{:S(2)}) copy-start(s32[32]{0:T(128)} %get-tuple-element.280) | copy-start | bytes 388 | tf_op jit(solution)/shard_map/cond
  84.6 6.4 %copy-start.37 = (s32[32,32]{1,0:T(8,128)S(1)}, s32[32,32]{1,0:T(8,128)}, u32[]{:S(2)}) copy-start(s32[32,32]{1,0:T(8,128)} %get-tuple-element.119) | copy-start | bytes 12292 | tf_op jit(solution)/shard_map/cond
  84.6 8.3 %copy-start.15 = (s32[32]{0:T(128)S(1)}, s32[32]{0:T(128)}, u32[]{:S(2)}) copy-start(s32[32]{0:T(128)} %get-tuple-element.284) | copy-start | bytes 388 | tf_op jit(solution)/shard_map/cond
  84.6 8.9 %copy-start.46 = (s32[4]{0:T(128)S(1)}, s32[4]{0:T(128)}, u32[]{:S(2)}) copy-start(s32[4]{0:T(128)} %copy-done.45) | copy-start | bytes 52 | tf_op jit(solution)/shard_map/cond
  86.9 13.5 %collective-permute-start.32 = (bf16[2,2,2,4,256,256]{5,4,3,2,1,0:T(8,128)(2,1)}, bf16[2,2,2,4,256,256]{5,4,3,2,1,0:T(8,128)(2,1)}, u32[]{:S(2)}, u32[]{:S(2)}) collective-permute-start(bf16[2,2,2,4,256,256]{5,4,3,2,1,0:T(8,128)(2,1)} %bitcast.18.refs_2_.refs_3_), channel_id=1, source_target_pairs={{0,1},{1,0},{2,3},{3,2},{4,5},{5,4},{6,7},{7,6},{8,9},{9,8},{10,11... | collective-permute-start | bytes 12582920 | tf_op jit(solution)/shard_map/cond/branch_1_fun/ppermute | solution.py:287
  89.0 24.1 %collective-permute-start.33 = (bf16[3,256,256]{2,1,0:T(8,128)(2,1)}, bf16[3,256,256]{2,1,0:T(8,128)(2,1)}, u32[]{:S(2)}, u32[]{:S(2)}) collective-permute-start(bf16[3,256,256]{2,1,0:T(8,128)(2,1)} %get-tuple-element.153), channel_id=1, source_target_pairs={{0,24},{8,16},{16,8},{24,0},{1,25},{9,17},{17,9},{25,1},{2,26},{10... | collective-permute-start | bytes 1179656 | tf_op jit(solution)/shard_map/cond/branch_1_fun/ppermute | solution.py:287
  93.6 37.4 %collective-permute-start.30 = (bf16[8,256,256]{2,1,0:T(8,128)(2,1)S(1)}, bf16[8,256,256]{2,1,0:T(8,128)(2,1)}, u32[]{:S(2)}, u32[]{:S(2)}) collective-permute-start(bf16[8,256,256]{2,1,0:T(8,128)(2,1)S(1)} %collective-permute-done.25.refs_0_), channel_id=1, source_target_pairs={{8,16},{16,8},{9,17},{17,9},{10,18},{18,10},{11,19},{19,11},{12,20... | collective-permute-start | bytes 3145736 | tf_op jit(solution)/shard_map/cond/branch_1_fun/ppermute | solution.py:280
  95.9 35.1 %collective-permute-start.31 = (bf16[8,256,256]{2,1,0:T(8,128)(2,1)}, bf16[8,256,256]{2,1,0:T(8,128)(2,1)S(1)}, u32[]{:S(2)}, u32[]{:S(2)}) collective-permute-start(bf16[8,256,256]{2,1,0:T(8,128)(2,1)} %copy-done.31), channel_id=1, source_target_pairs={{8,0},{16,24},{9,1},{17,25},{10,2},{18,26},{11,3},{19,27},{12,4},{... | collective-permute-start | bytes 3145736 | tf_op jit(solution)/shard_map/cond/branch_1_fun/ppermute | solution.py:283
  105.2 38.1 %copy-start.5 = (bf16[3,256,256]{2,1,0:T(8,128)(2,1)S(1)}, bf16[3,256,256]{2,1,0:T(8,128)(2,1)}, u32[]{:S(2)}) copy-start(bf16[3,256,256]{2,1,0:T(8,128)(2,1)} %copy-done.4) | copy-start | bytes 1179652 | tf_op jit(solution)/shard_map/cond
  131.0 32.9 %collective-permute-start.35 = (bf16[3,256,256]{2,1,0:T(8,128)(2,1)}, bf16[3,256,256]{2,1,0:T(8,128)(2,1)S(1)}, u32[]{:S(2)}, u32[]{:S(2)}) collective-permute-start(bf16[3,256,256]{2,1,0:T(8,128)(2,1)} %get-tuple-element.160), channel_id=1, source_target_pairs={{0,24},{8,16},{16,8},{24,0},{1,25},{9,17},{17,9},{25,1},{2,26},{10... | collective-permute-start | bytes 1179656 | tf_op jit(solution)/shard_map/cond/branch_1_fun/ppermute | solution.py:287
  140.5 23.3 %collective-permute-start.34 = (bf16[8,256,256]{2,1,0:T(8,128)(2,1)}, bf16[8,256,256]{2,1,0:T(8,128)(2,1)S(1)}, u32[]{:S(2)}, u32[]{:S(2)}) collective-permute-start(bf16[8,256,256]{2,1,0:T(8,128)(2,1)} %collective-permute-done.30), channel_id=1, source_target_pairs={{8,0},{16,24},{9,1},{17,25},{10,2},{18,26},{11,3},{19,27},{12,4},{... | collective-permute-start | bytes 3145736 | tf_op jit(solution)/shard_map/cond/branch_1_fun/ppermute | solution.py:283
  150.3 13.5 %copy-start.32 = (bf16[8,256,256]{2,1,0:T(8,128)(2,1)S(1)}, bf16[8,256,256]{2,1,0:T(8,128)(2,1)}, u32[]{:S(2)}) copy-start(bf16[8,256,256]{2,1,0:T(8,128)(2,1)} %copy-done.31) | copy-start | bytes 3145732 | tf_op jit(solution)/shard_map/cond
  150.3 33.8 %all-to-all-start.2 = ((bf16[4,4,256,256]{3,2,1,0:T(8,128)(2,1)}), bf16[4,4,256,256]{3,2,1,0:T(8,128)(2,1)}, u32[]{:S(2)}, u32[]{:S(2)}) async-start(bf16[4,4,256,256]{3,2,1,0:T(8,128)(2,1)} %bitcast.19), calls=%async_computation.2 | async-start | bytes 4194304 | tf_op jit(solution)/shard_map/cond/branch_1_fun/all_to_all | solution.py:335
  184.1 28.0 %all-to-all-start.3 = ((bf16[4,4,256,256]{3,2,1,0:T(8,128)(2,1)}), bf16[4,4,256,256]{3,2,1,0:T(8,128)(2,1)S(1)}, u32[]{:S(2)}, u32[]{:S(2)}) async-start(bf16[4,4,256,256]{3,2,1,0:T(8,128)(2,1)} %bitcast.20), calls=%async_computation.3 | async-start | bytes 4194304 | tf_op jit(solution)/shard_map/cond/branch_1_fun/all_to_all | solution.py:335
  187.7 25.8 %collective-permute-start.36 = (bf16[4,4,256,256]{3,2,1,0:T(8,128)(2,1)}, bf16[4,4,256,256]{3,2,1,0:T(8,128)(2,1)}, u32[]{:S(2)}, u32[]{:S(2)}) collective-permute-start(bf16[4,4,256,256]{3,2,1,0:T(8,128)(2,1)} %all-to-all-done.2.refs_0_), channel_id=1, source_target_pairs={{0,1},{1,0},{2,3},{3,2},{4,5},{5,4},{6,7},{7,6},{8,9},{9,8},{10,11... | collective-permute-start | bytes 6291464 | tf_op jit(solution)/shard_map/cond/branch_1_fun/ppermute | solution.py:287
  212.2 5.3 %collective-permute-start.37 = (bf16[4,4,256,256]{3,2,1,0:T(8,128)(2,1)S(1)}, bf16[4,4,256,256]{3,2,1,0:T(8,128)(2,1)}, u32[]{:S(2)}, u32[]{:S(2)}) collective-permute-start(bf16[4,4,256,256]{3,2,1,0:T(8,128)(2,1)S(1)} %all-to-all-done.3.refs_1_), channel_id=1, source_target_pairs={{0,1},{1,0},{2,3},{3,2},{4,5},{5,4},{6,7},{7,6},{8,9},{9,8},{10,11... | collective-permute-start | bytes 6291464 | tf_op jit(solution)/shard_map/cond/branch_1_fun/ppermute | solution.py:287
  (4 other events, 12.0 us)

commit v4 on v3

--- a/solution.py
+++ b/solution.py
@@ -200,6 +200,8 @@
     out = []
     for d, many in PIECES.items():
         ends = [-(-room * at // many) for at in range(many + 1)]
+        if many > 1:
+            ends[1] += 1
         out += [(d, first, end - first) for first, end in zip(ends[:-1], ends[1:])]
     return out
 

time: 222 us -> 218 us (0.982)
  starting transfers between devices: 46.5 us -> 36.6 us
  Pallas kernels: 38.9 us -> 44.8 us
    all_to_all x2, waiting for transfers between devices: 36.8 us -> 27 us  [planned(): lax.all_to_all(done, ('y', 'x'), split_axis=0, concat_axis=0, tiled=True)]
    ppermute x15, starting transfers between devices: 25.5 us -> 18.2 us  [flip(): return lax.ppermute(value, axis, [(i, i ^ bit) for i in range(size)])]
    pallas_call x4, Pallas kernels: 27 us -> 32.4 us  [multiply(): pl.pallas_call(body, grid_spec=pltpu.PrefetchScalarGridSpec(num_scalar_pr...]
    ppermute x2, waiting for transfers between devices: 17.8 us -> 22.5 us  [inner(): return lax.ppermute(value, 'z', [(1, 2), (2, 1)])]
    ppermute x2, waiting for transfers between devices: 6.76 us -> 9.9 us  [outer(): return lax.ppermute(value, 'z', [(1, 0), (2, 3)])]
  transfers between devices with their start and end apart: 21 -> 21, of which waited for: 7 -> 9; matrix products, arithmetic and copies ran while one was open for 3% -> 3% of each run, Pallas kernels for 12% -> 15%
where the time goes in v4:
time: 218 us
  waiting for transfers between devices  120 us (55%)
  Pallas kernels  44.8 us (21%)
  starting transfers between devices  36.6 us (17%)
  other arithmetic  9.8 us (4%)
  local copies, waits for them, and re-layouts  6.3 us (3%)
    ppermute x15, waiting for transfers between devices, flip(): return lax.ppermute(value, axis, [(i, i ^ bit) for i in range(size)])  60.2 us
    pallas_call x4, Pallas kernels, multiply(): pl.pallas_call(body, grid_spec=pltpu.PrefetchScalarGridSpec(num_scalar_pr...  32.4 us
    all_to_all x2, waiting for transfers between devices, planned(): lax.all_to_all(done, ('y', 'x'), split_axis=0, concat_axis=0, tiled=True)  27 us
    ppermute x2, waiting for transfers between devices, inner(): return lax.ppermute(value, 'z', [(1, 2), (2, 1)])  22.5 us
    ppermute x15, starting transfers between devices, flip(): return lax.ppermute(value, axis, [(i, i ^ bit) for i in range(size)])  18.2 us
    ppermute x2, waiting for transfers between devices, outer(): return lax.ppermute(value, 'z', [(1, 0), (2, 3)])  9.9 us
    all_to_all x2, starting transfers between devices, planned(): lax.all_to_all(done, ('y', 'x'), split_axis=0, concat_axis=0, tiled=True)  8.17 us
    pallas_call x1, Pallas kernels, cut_out(): pl.pallas_call(body, grid_spec=pltpu.PrefetchScalarGridSpec(num_scalar_pr...  6.85 us
  transfers between devices with their start and end apart: 21, of which 9 were waited for; matrix products, arithmetic and copies ran while one was open for 3% of the time, Pallas kernels for 15%

profile of v4, /device:TPU:9, one launch (start us, length us, event | category | flops | bytes accessed | tf_op | source)
XLA Modules:
  0.0 218.0 jit_solution(8957485773941764965)
XLA Ops:
  2.9 1.9 fusion.8
  5.5 212.5 %conditional.1 = (bf16[8,4,256,256]{3,2,1,0:T(8,128)(2,1)}) conditional(s32[]{:T(128)} %clamp.3, (s32[32,32]{1,0:T(8,128)}, s32[32]{0:T(128)}, s32[32]{0:T(128)}, s32[4]{0:T(128)S(1)}, s32[8,8]{1,0:T(8,128)S(1)}, /*index=5*/bf16[4,32,256,256]{3,2,1,0:T(8,128)(2,1)}, bf16[2,4,256,256]{3,2,1,0:T(8,128)(2,1)}, ...), branch_computations={%region_5.9_spmd, %region_9.13_spmd, %region_13.17_spmd, %region_1... | conditional | flops 68727611392 | bytes 198736160 | solution.py:401
  6.6 6.8 %branch_1_fun.6 = (bf16[6,256,256]{2,1,0:T(8,128)(2,1)}, bf16[4,256,256]{2,1,0:T(8,128)(2,1)}, bf16[2,256,256]{2,1,0:T(8,128)(2,1)}, bf16[4,256,256]{2,1,0:T(8,1...) custom-call(s32[24]{0:T(128)} %reshape.561.c_ref, ...), custom_call_target="tpu_custom_call" | custom-call | tf_op jit(solution)/shard_map/cond/branch_1_fun/pallas_call | solution.py:241
  13.7 2.3 %collective-permute-start.24 = (bf16[4,256,256]{2,1,0:T(8,128)(2,1)}, bf16[4,256,256]{2,1,0:T(8,128)(2,1)S(1)}, u32[]{:S(2)}, u32[]{:S(2)}) collective-permute-start(bf16[4,256,256]{2,1,0:T(8,128)(2,1)} %get-tuple-element.139), channel_id=1, source_target_pairs={{0,16},{8,24},{16,0},{24,8},{1,17},{9,25},{17,1},{25,9},{2,18},{10... | collective-permute-start | bytes 1572872 | tf_op jit(solution)/shard_map/cond/branch_1_fun/ppermute | solution.py:289
  17.8 1.4 collective-permute-start.22
  20.5 18.4 %collective-permute-done.24.refs_1_ = bf16[4,256,256]{2,1,0:T(8,128)(2,1)S(1)} collective-permute-done((bf16[4,256,256]{2,1,0:T(8,128)(2,1)}, bf16[4,256,256]{2,1,0:T(8,128)(2,1)S(1)}, u32[]{:S(2)}, u32[]{:S(2)}) %collective-permute-start.24) | collective-permute-done | bytes 524320 | tf_op jit(solution)/shard_map/cond/branch_1_fun/ppermute | solution.py:289
  38.9 6.8 %collective-permute-done.23.refs_1_ = bf16[6,256,256]{2,1,0:T(8,128)(2,1)S(1)} collective-permute-done((bf16[6,256,256]{2,1,0:T(8,128)(2,1)}, bf16[6,256,256]{2,1,0:T(8,128)(2,1)S(1)}, u32[]{:S(2)}, u32[]{:S(2)}) %collective-permute-start.23) | collective-permute-done | bytes 786464 | tf_op jit(solution)/shard_map/cond/branch_1_fun/ppermute | solution.py:289
  45.8 2.1 collective-permute-start.26
  48.0 1.8 collective-permute-start.28
  49.8 2.2 %collective-permute-start.29 = (bf16[2,256,256]{2,1,0:T(8,128)(2,1)S(1)}, bf16[2,256,256]{2,1,0:T(8,128)(2,1)S(1)}, u32[]{:S(2)}, u32[]{:S(2)}) collective-permute-start(bf16[2,256,256]{2,1,0:T(8,128)(2,1)S(1)} %copy-done.46), channel_id=1, source_target_pairs={{0,16},{8,24},{16,0},{24,8},{1,17},{9,25},{17,1},{25,9},{2,18},{10... | collective-permute-start | bytes 786440 | tf_op jit(solution)/shard_map/cond/branch_1_fun/ppermute | solution.py:289
  52.0 28.7 %collective-permute-done.29.refs_2_ = bf16[2,256,256]{2,1,0:T(8,128)(2,1)S(1)} collective-permute-done((bf16[2,256,256]{2,1,0:T(8,128)(2,1)S(1)}, bf16[2,256,256]{2,1,0:T(8,128)(2,1)S(1)}, u32[]{:S(2)}, u32[]{:S(2)}) %collective-permute-start.29) | collective-permute-done | bytes 262176 | tf_op jit(solution)/shard_map/cond/branch_1_fun/ppermute | solution.py:289
  81.5 2.1 collective-permute-done.27
  84.7 2.3 %pad_maximum_fusion.2 = bf16[4,2,4,256,256]{4,3,2,1,0:T(8,128)(2,1)} fusion(bf16[1,2,4,256,256]{4,3,2,1,0:T(8,128)(2,1)S(1)} %bitcast.78, bf16[1,2,4,256,256]{4,3,2,1,0:T(8,128)(2,1)S(1)} %bitcast.74, bf16[1,2,4,256,256]{4,3,2,1,0:T(8,128)(2,1)S(1)} %maximum_bitcast_fusion.1, bf16[1,2,4,256,256]{4,3,2,1,0:T(8,128)(2,1)S(1)} %bitcast.66), kind=kLoop, calls=%fused_computation.47 | loop fusion | flops 6291456 | bytes 8388608 | tf_op jit(solution)/shard_map/cond/branch_1_fun/stack | solution.py:315
  87.0 1.5 collective-permute-start.32
  93.2 2.2 collective-permute-start.30
  95.4 3.7 %collective-permute-start.31 = (bf16[8,256,256]{2,1,0:T(8,128)(2,1)}, bf16[8,256,256]{2,1,0:T(8,128)(2,1)S(1)}, u32[]{:S(2)}, u32[]{:S(2)}) collective-permute-start(bf16[8,256,256]{2,1,0:T(8,128)(2,1)} %copy-done.28), channel_id=1, source_target_pairs={{8,0},{16,24},{9,1},{17,25},{10,2},{18,26},{11,3},{19,27},{12,4},{... | collective-permute-start | bytes 3145736 | tf_op jit(solution)/shard_map/cond/branch_1_fun/ppermute | solution.py:285
  99.1 7.4 %branch_1_fun.7.refs_5_ = bf16[2,2,4,256,256]{4,3,2,1,0:T(8,128)(2,1)} custom-call(s32[112]{0:T(128)S(1)} %concatenate.36.s_ref, bf16[8,256,256]{2,1,0:T(8,128)(2,1)S(1)} %constant_dynamic-update-slice_fusion.3.refs_0_, bf16[4,32,256,256]{3,2,1,0:T(8,128)(2,1)} %get-tuple-element.300.refs_0_.refs_1_.refs_2_.refs_3_.refs_4_, ...), custom_call_target="tpu_custom_call" | custom-call | flops 17179869184 | bytes 11534336 | tf_op jit(solution)/shard_map/cond/branch_1_fun/pallas_call | solution.py:142
  106.5 7.1 %branch_1_fun.8.refs_5_ = bf16[2,2,4,256,256]{4,3,2,1,0:T(8,128)(2,1)} custom-call(s32[112]{0:T(128)S(1)} %concatenate.36.s_ref, bf16[8,256,256]{2,1,0:T(8,128)(2,1)S(1)} %collective-permute-done.25.refs_0_, bf16[6,256,256]{2,1,0:T(8,128)(2,1)S(1)} %collective-permute-done.23.refs_1_, bf16[2,2,2,4,256,256]{5,4,3,2,1,0:T(8,128)(2,1)} %bitcast.18.refs_2_.refs_3_, ...), custom_call_target="tpu_custom_call" | custom-call | flops 17179869184 | bytes 11534336 | tf_op jit(solution)/shard_map/cond/branch_1_fun/pallas_call | solution.py:142
  113.6 22.5 %collective-permute-done.30 = bf16[8,256,256]{2,1,0:T(8,128)(2,1)} collective-permute-done((bf16[8,256,256]{2,1,0:T(8,128)(2,1)S(1)}, bf16[8,256,256]{2,1,0:T(8,128)(2,1)}, u32[]{:S(2)}, u32[]{:S(2)}) %collective-permute-start.30) | collective-permute-done | bytes 1048608 | tf_op jit(solution)/shard_map/cond/branch_1_fun/ppermute | solution.py:282
  136.1 2.3 %collective-permute-start.34 = (bf16[8,256,256]{2,1,0:T(8,128)(2,1)}, bf16[8,256,256]{2,1,0:T(8,128)(2,1)}, u32[]{:S(2)}, u32[]{:S(2)}) collective-permute-start(bf16[8,256,256]{2,1,0:T(8,128)(2,1)} %collective-permute-done.30), channel_id=1, source_target_pairs={{8,0},{16,24},{9,1},{17,25},{10,2},{18,26},{11,3},{19,27},{12,4},{... | collective-permute-start | bytes 3145736 | tf_op jit(solution)/shard_map/cond/branch_1_fun/ppermute | solution.py:285
  138.4 1.3 broadcast_select_fusion.4.refs_0_
  139.7 8.6 %branch_1_fun.9 = bf16[2,2,4,256,256]{4,3,2,1,0:T(8,128)(2,1)} custom-call(s32[112]{0:T(128)S(1)} %concatenate.36.s_ref, bf16[8,256,256]{2,1,0:T(8,128)(2,1)S(1)} %broadcast_select_fusion.4.refs_0_, bf16[4,256,256]{2,1,0:T(8,128)(2,1)S(1)} %collective-permute-done.24.refs_1_, bf16[2,256,256]{2,1,0:T(8,128)(2,1)S(1)} %copy-done.5, ...), custom_call_target="tpu_custom_call", output_to_operand_aliasing={{}: (6, {})} | custom-call | flops 17179869184 | bytes 11534336 | tf_op jit(solution)/shard_map/cond/branch_1_fun/pallas_call | solution.py:142
  148.4 3.7 %all-to-all-start.2 = ((bf16[4,4,256,256]{3,2,1,0:T(8,128)(2,1)}), bf16[4,4,256,256]{3,2,1,0:T(8,128)(2,1)S(1)}, u32[]{:S(2)}, u32[]{:S(2)}) async-start(bf16[4,4,256,256]{3,2,1,0:T(8,128)(2,1)} %bitcast.19), calls=%async_computation.2 | async-start | bytes 4194304 | tf_op jit(solution)/shard_map/cond/branch_1_fun/all_to_all | solution.py:337
  152.1 3.3 %collective-permute-start.35 = (bf16[2,256,256]{2,1,0:T(8,128)(2,1)S(1)}, bf16[2,256,256]{2,1,0:T(8,128)(2,1)S(1)}, u32[]{:S(2)}, u32[]{:S(2)}) collective-permute-start(bf16[2,256,256]{2,1,0:T(8,128)(2,1)S(1)} %copy-done.44), channel_id=1, source_target_pairs={{0,24},{8,16},{16,8},{24,0},{1,25},{9,17},{17,9},{25,1},{2,26},{10... | collective-permute-start | bytes 786440 | tf_op jit(solution)/shard_map/cond/branch_1_fun/ppermute | solution.py:289
  155.4 9.9 %collective-permute-done.34 = bf16[8,256,256]{2,1,0:T(8,128)(2,1)} collective-permute-done((bf16[8,256,256]{2,1,0:T(8,128)(2,1)}, bf16[8,256,256]{2,1,0:T(8,128)(2,1)}, u32[]{:S(2)}, u32[]{:S(2)}) %collective-permute-start.34) | collective-permute-done | bytes 1048608 | tf_op jit(solution)/shard_map/cond/branch_1_fun/ppermute | solution.py:285
  165.5 9.3 %branch_1_fun.10 = bf16[2,2,4,256,256]{4,3,2,1,0:T(8,128)(2,1)} custom-call(s32[112]{0:T(128)S(1)} %concatenate.36.s_ref, bf16[8,256,256]{2,1,0:T(8,128)(2,1)S(1)} %broadcast_select_fusion.3.refs_0_, bf16[4,256,256]{2,1,0:T(8,128)(2,1)} %collective-permute-done.33.refs_1_, ...), custom_call_target="tpu_custom_call", output_to_operand_aliasing={{}: (6, {})} | custom-call | flops 17179869184 | bytes 11534336 | tf_op jit(solution)/shard_map/cond/branch_1_fun/pallas_call | solution.py:142
  174.8 3.2 %all-to-all-done.2.refs_0_ = bf16[4,4,256,256]{3,2,1,0:T(8,128)(2,1)S(1)} async-done(((bf16[4,4,256,256]{3,2,1,0:T(8,128)(2,1)}), bf16[4,4,256,256]{3,2,1,0:T(8,128)(2,1)S(1)}, u32[]{:S(2)}, u32[]{:S(2)}) %all-to-all-start.2) | async-done | bytes 2097184 | tf_op jit(solution)/shard_map/cond/branch_1_fun/all_to_all | solution.py:337
  178.0 4.4 %all-to-all-start.3 = ((bf16[4,4,256,256]{3,2,1,0:T(8,128)(2,1)}), bf16[4,4,256,256]{3,2,1,0:T(8,128)(2,1)}, u32[]{:S(2)}, u32[]{:S(2)}) async-start(bf16[4,4,256,256]{3,2,1,0:T(8,128)(2,1)} %bitcast.20), calls=%async_computation.3 | async-start | bytes 4194304 | tf_op jit(solution)/shard_map/cond/branch_1_fun/all_to_all | solution.py:337
  183.1 23.7 %all-to-all-done.3.refs_1_ = bf16[4,4,256,256]{3,2,1,0:T(8,128)(2,1)} async-done(((bf16[4,4,256,256]{3,2,1,0:T(8,128)(2,1)}), bf16[4,4,256,256]{3,2,1,0:T(8,128)(2,1)}, u32[]{:S(2)}, u32[]{:S(2)}) %all-to-all-start.3) | async-done | bytes 2097184 | tf_op jit(solution)/shard_map/cond/branch_1_fun/all_to_all | solution.py:337
  206.9 1.4 collective-permute-start.37
  208.3 4.1 %collective-permute-done.37.refs_3_ = bf16[4,4,256,256]{3,2,1,0:T(8,128)(2,1)} collective-permute-done((bf16[4,4,256,256]{3,2,1,0:T(8,128)(2,1)}, bf16[4,4,256,256]{3,2,1,0:T(8,128)(2,1)}, u32[]{:S(2)}, u32[]{:S(2)}) %collective-permute-start.37) | collective-permute-done | bytes 2097184 | tf_op jit(solution)/shard_map/cond/branch_1_fun/ppermute | solution.py:289
  212.5 5.6 %branch_1_fun.11 = bf16[4,2,4,256,256]{4,3,2,1,0:T(8,128)(2,1)} custom-call(s32[4]{0:T(128)S(1)} %get-tuple-element.118.s_ref, bf16[4,4,256,256]{3,2,1,0:T(8,128)(2,1)} %copy-done.23, bf16[4,4,256,256]{3,2,1,0:T(8,128)(2,1)} %all-to-all-done.3.refs_1_, bf16[4,4,256,256]{3,2,1,0:T(8,128)(2,1)} %collective-permute-done.36.refs_2_, ...), custom_call_target="tpu_custom_call" | custom-call | tf_op jit(solution)/shard_map/cond/branch_1_fun/pallas_call | solution.py:182
  (107 shorter events, 14.8 us)
Async XLA Ops:
  6.6 9.9 %copy-start.16 = (bf16[2,4,256,256]{3,2,1,0:T(8,128)(2,1)S(1)}, bf16[2,4,256,256]{3,2,1,0:T(8,128)(2,1)}, u32[]{:S(2)}) copy-start(bf16[2,4,256,256]{3,2,1,0:T(8,128)(2,1)} %get-tuple-element.137) | copy-start | bytes 3145732 | tf_op jit(solution)/shard_map/cond
  13.5 32.2 %copy-start.38 = (bf16[2,256,256]{2,1,0:T(8,128)(2,1)S(1)}, bf16[2,256,256]{2,1,0:T(8,128)(2,1)}, u32[]{:S(2)}) copy-start(bf16[2,256,256]{2,1,0:T(8,128)(2,1)} %get-tuple-element.140) | copy-start | bytes 786436 | tf_op jit(solution)/shard_map/cond
  13.5 36.3 %copy-start.46 = (bf16[2,256,256]{2,1,0:T(8,128)(2,1)S(1)}, bf16[2,256,256]{2,1,0:T(8,128)(2,1)}, u32[]{:S(2)}) copy-start(bf16[2,256,256]{2,1,0:T(8,128)(2,1)} %get-tuple-element.145) | copy-start | bytes 786436 | tf_op jit(solution)/shard_map/cond
  13.5 71.2 %copy-start.17 = (bf16[2,4,256,256]{3,2,1,0:T(8,128)(2,1)S(1)}, bf16[2,4,256,256]{3,2,1,0:T(8,128)(2,1)}, u32[]{:S(2)}) copy-start(bf16[2,4,256,256]{3,2,1,0:T(8,128)(2,1)} %get-tuple-element.137) | copy-start | bytes 3145732 | tf_op jit(solution)/shard_map/cond
  13.5 5.7 %collective-permute-start.19 = (bf16[4,256,256]{2,1,0:T(8,128)(2,1)}, bf16[4,256,256]{2,1,0:T(8,128)(2,1)S(1)}, u32[]{:S(2)}, u32[]{:S(2)}) collective-permute-start(bf16[4,256,256]{2,1,0:T(8,128)(2,1)} %get-tuple-element.135), channel_id=1, source_target_pairs={{0,1},{1,0},{2,3},{3,2},{4,5},{5,4},{6,7},{7,6},{8,9},{9,8},{10,11... | collective-permute-start | bytes 1572872 | tf_op jit(solution)/shard_map/cond/branch_1_fun/ppermute | solution.py:289
  13.7 25.2 %collective-permute-start.24 = (bf16[4,256,256]{2,1,0:T(8,128)(2,1)}, bf16[4,256,256]{2,1,0:T(8,128)(2,1)S(1)}, u32[]{:S(2)}, u32[]{:S(2)}) collective-permute-start(bf16[4,256,256]{2,1,0:T(8,128)(2,1)} %get-tuple-element.139), channel_id=1, source_target_pairs={{0,16},{8,24},{16,0},{24,8},{1,17},{9,25},{17,1},{25,9},{2,18},{10... | collective-permute-start | bytes 1572872 | tf_op jit(solution)/shard_map/cond/branch_1_fun/ppermute | solution.py:289
  15.9 29.7 %collective-permute-start.23 = (bf16[6,256,256]{2,1,0:T(8,128)(2,1)}, bf16[6,256,256]{2,1,0:T(8,128)(2,1)S(1)}, u32[]{:S(2)}, u32[]{:S(2)}) collective-permute-start(bf16[6,256,256]{2,1,0:T(8,128)(2,1)} %get-tuple-element.138), channel_id=1, source_target_pairs={{0,8},{8,0},{16,24},{24,16},{1,9},{9,1},{17,25},{25,17},{2,10},{10... | collective-permute-start | bytes 2359304 | tf_op jit(solution)/shard_map/cond/branch_1_fun/ppermute | solution.py:289
  16.5 29.1 %collective-permute-start.21 = (bf16[2,4,256,256]{3,2,1,0:T(8,128)(2,1)S(1)}, bf16[2,4,256,256]{3,2,1,0:T(8,128)(2,1)S(1)}, u32[]{:S(2)}, u32[]{:S(2)}) collective-permute-start(bf16[2,4,256,256]{3,2,1,0:T(8,128)(2,1)S(1)} %copy-done.16), channel_id=1, source_target_pairs={{0,4},{4,0},{1,5},{5,1},{2,6},{6,2},{3,7},{7,3},{8,12},{12,8},{9,1... | collective-permute-start | bytes 3145736 | tf_op jit(solution)/shard_map/cond/branch_1_fun/ppermute | solution.py:289
  17.8 21.1 %collective-permute-start.22 = (bf16[1,4,256,256]{3,2,1,0:T(8,128)(2,1)S(1)}, bf16[1,4,256,256]{3,2,1,0:T(8,128)(2,1)S(1)}, u32[]{:S(2)}, u32[]{:S(2)}) collective-permute-start(bf16[1,4,256,256]{3,2,1,0:T(8,128)(2,1)S(1)} %get-tuple-element.463), channel_id=1, source_target_pairs={{0,2},{2,0},{1,3},{3,1},{4,6},{6,4},{5,7},{7,5},{8,10},{10,8},{9,1... | collective-permute-start | bytes 1572872 | tf_op jit(solution)/shard_map/cond/branch_1_fun/ppermute | solution.py:289
  20.3 25.4 %collective-permute-start.20 = (bf16[4,256,256]{2,1,0:T(8,128)(2,1)S(1)}, bf16[4,256,256]{2,1,0:T(8,128)(2,1)S(1)}, u32[]{:S(2)}, u32[]{:S(2)}) collective-permute-start(bf16[4,256,256]{2,1,0:T(8,128)(2,1)S(1)} %pad_maximum_fusion.3), channel_id=1, source_target_pairs={{0,2},{2,0},{1,3},{3,1},{4,6},{6,4},{5,7},{7,5},{8,10},{10,8},{9,1... | collective-permute-start | bytes 1572872 | tf_op jit(solution)/shard_map/cond/branch_1_fun/ppermute | solution.py:289
  45.8 37.8 %collective-permute-start.26 = (bf16[8,256,256]{2,1,0:T(8,128)(2,1)S(1)}, bf16[8,256,256]{2,1,0:T(8,128)(2,1)S(1)}, u32[]{:S(2)}, u32[]{:S(2)}) collective-permute-start(bf16[8,256,256]{2,1,0:T(8,128)(2,1)S(1)} %constant_dynamic-update-slice_fusion.3.refs_0_), channel_id=1, source_target_pairs={{8,16},{16,8},{9,17},{17,9},{10,18},{18,10},{11,19},{19,11},{12,20... | collective-permute-start | bytes 3145736 | tf_op jit(solution)/shard_map/cond/branch_1_fun/ppermute | solution.py:282
  47.9 35.7 %collective-permute-start.25 = (bf16[8,256,256]{2,1,0:T(8,128)(2,1)S(1)}, bf16[8,256,256]{2,1,0:T(8,128)(2,1)S(1)}, u32[]{:S(2)}, u32[]{:S(2)}) collective-permute-start(bf16[8,256,256]{2,1,0:T(8,128)(2,1)S(1)} %constant_dynamic-update-slice_fusion.3.refs_0_), channel_id=1, source_target_pairs={{0,8},{8,0},{16,24},{24,16},{1,9},{9,1},{17,25},{25,17},{2,10},{10... | collective-permute-start | bytes 3145736 | tf_op jit(solution)/shard_map/cond/branch_1_fun/ppermute | solution.py:289
  48.0 36.6 %collective-permute-start.28 = (bf16[2,4,256,256]{3,2,1,0:T(8,128)(2,1)S(1)}, bf16[2,4,256,256]{3,2,1,0:T(8,128)(2,1)S(1)}, u32[]{:S(2)}, u32[]{:S(2)}) collective-permute-start(bf16[2,4,256,256]{3,2,1,0:T(8,128)(2,1)S(1)} %collective-permute-done.21), channel_id=1, source_target_pairs={{0,2},{2,0},{1,3},{3,1},{4,6},{6,4},{5,7},{7,5},{8,10},{10,8},{9,1... | collective-permute-start | bytes 3145736 | tf_op jit(solution)/shard_map/cond/branch_1_fun/ppermute | solution.py:289
  49.7 33.8 %collective-permute-start.27 = (bf16[1,4,256,256]{3,2,1,0:T(8,128)(2,1)S(1)}, bf16[1,4,256,256]{3,2,1,0:T(8,128)(2,1)S(1)}, u32[]{:S(2)}, u32[]{:S(2)}) collective-permute-start(bf16[1,4,256,256]{3,2,1,0:T(8,128)(2,1)S(1)} %get-tuple-element.143), channel_id=1, source_target_pairs={{0,2},{2,0},{1,3},{3,1},{4,6},{6,4},{5,7},{7,5},{8,10},{10,8},{9,1... | collective-permute-start | bytes 1572872 | tf_op jit(solution)/shard_map/cond/branch_1_fun/ppermute | solution.py:289
  49.8 31.0 %collective-permute-start.29 = (bf16[2,256,256]{2,1,0:T(8,128)(2,1)S(1)}, bf16[2,256,256]{2,1,0:T(8,128)(2,1)S(1)}, u32[]{:S(2)}, u32[]{:S(2)}) collective-permute-start(bf16[2,256,256]{2,1,0:T(8,128)(2,1)S(1)} %copy-done.46), channel_id=1, source_target_pairs={{0,16},{8,24},{16,0},{24,8},{1,17},{9,25},{17,1},{25,9},{2,18},{10... | collective-permute-start | bytes 786440 | tf_op jit(solution)/shard_map/cond/branch_1_fun/ppermute | solution.py:289
  84.7 5.3 %copy-start.7 = (s32[32]{0:T(128)S(1)}, s32[32]{0:T(128)}, u32[]{:S(2)}) copy-start(s32[32]{0:T(128)} %get-tuple-element.280) | copy-start | bytes 388 | tf_op jit(solution)/shard_map/cond
  84.7 5.9 %copy-start.35 = (s32[32,32]{1,0:T(8,128)S(1)}, s32[32,32]{1,0:T(8,128)}, u32[]{:S(2)}) copy-start(s32[32,32]{1,0:T(8,128)} %get-tuple-element.119) | copy-start | bytes 12292 | tf_op jit(solution)/shard_map/cond
  84.7 7.8 %copy-start.11 = (s32[32]{0:T(128)S(1)}, s32[32]{0:T(128)}, u32[]{:S(2)}) copy-start(s32[32]{0:T(128)} %get-tuple-element.284) | copy-start | bytes 388 | tf_op jit(solution)/shard_map/cond
  87.0 12.1 %collective-permute-start.32 = (bf16[2,2,2,4,256,256]{5,4,3,2,1,0:T(8,128)(2,1)}, bf16[2,2,2,4,256,256]{5,4,3,2,1,0:T(8,128)(2,1)}, u32[]{:S(2)}, u32[]{:S(2)}) collective-permute-start(bf16[2,2,2,4,256,256]{5,4,3,2,1,0:T(8,128)(2,1)} %bitcast.18.refs_2_.refs_3_), channel_id=1, source_target_pairs={{0,1},{1,0},{2,3},{3,2},{4,5},{5,4},{6,7},{7,6},{8,9},{9,8},{10,11... | collective-permute-start | bytes 12582920 | tf_op jit(solution)/shard_map/cond/branch_1_fun/ppermute | solution.py:289
  88.5 25.1 %collective-permute-start.33 = (bf16[4,256,256]{2,1,0:T(8,128)(2,1)}, bf16[4,256,256]{2,1,0:T(8,128)(2,1)}, u32[]{:S(2)}, u32[]{:S(2)}) collective-permute-start(bf16[4,256,256]{2,1,0:T(8,128)(2,1)} %get-tuple-element.153), channel_id=1, source_target_pairs={{0,24},{8,16},{16,8},{24,0},{1,25},{9,17},{17,9},{25,1},{2,26},{10... | collective-permute-start | bytes 1572872 | tf_op jit(solution)/shard_map/cond/branch_1_fun/ppermute | solution.py:289
  93.2 42.9 %collective-permute-start.30 = (bf16[8,256,256]{2,1,0:T(8,128)(2,1)S(1)}, bf16[8,256,256]{2,1,0:T(8,128)(2,1)}, u32[]{:S(2)}, u32[]{:S(2)}) collective-permute-start(bf16[8,256,256]{2,1,0:T(8,128)(2,1)S(1)} %collective-permute-done.25.refs_0_), channel_id=1, source_target_pairs={{8,16},{16,8},{9,17},{17,9},{10,18},{18,10},{11,19},{19,11},{12,20... | collective-permute-start | bytes 3145736 | tf_op jit(solution)/shard_map/cond/branch_1_fun/ppermute | solution.py:282
  95.4 40.7 %collective-permute-start.31 = (bf16[8,256,256]{2,1,0:T(8,128)(2,1)}, bf16[8,256,256]{2,1,0:T(8,128)(2,1)S(1)}, u32[]{:S(2)}, u32[]{:S(2)}) collective-permute-start(bf16[8,256,256]{2,1,0:T(8,128)(2,1)} %copy-done.28), channel_id=1, source_target_pairs={{8,0},{16,24},{9,1},{17,25},{10,2},{18,26},{11,3},{19,27},{12,4},{... | collective-permute-start | bytes 3145736 | tf_op jit(solution)/shard_map/cond/branch_1_fun/ppermute | solution.py:285
  106.5 33.2 %copy-start.5 = (bf16[2,256,256]{2,1,0:T(8,128)(2,1)S(1)}, bf16[2,256,256]{2,1,0:T(8,128)(2,1)}, u32[]{:S(2)}) copy-start(bf16[2,256,256]{2,1,0:T(8,128)(2,1)} %copy-done.4) | copy-start | bytes 786436 | tf_op jit(solution)/shard_map/cond
  136.1 29.2 %collective-permute-start.34 = (bf16[8,256,256]{2,1,0:T(8,128)(2,1)}, bf16[8,256,256]{2,1,0:T(8,128)(2,1)}, u32[]{:S(2)}, u32[]{:S(2)}) collective-permute-start(bf16[8,256,256]{2,1,0:T(8,128)(2,1)} %collective-permute-done.30), channel_id=1, source_target_pairs={{8,0},{16,24},{9,1},{17,25},{10,2},{18,26},{11,3},{19,27},{12,4},{... | collective-permute-start | bytes 3145736 | tf_op jit(solution)/shard_map/cond/branch_1_fun/ppermute | solution.py:285
  148.4 3.8 %copy-start.44 = (bf16[2,256,256]{2,1,0:T(8,128)(2,1)S(1)}, bf16[2,256,256]{2,1,0:T(8,128)(2,1)}, u32[]{:S(2)}) copy-start(bf16[2,256,256]{2,1,0:T(8,128)(2,1)} %get-tuple-element.160) | copy-start | bytes 786436 | tf_op jit(solution)/shard_map/cond
  148.4 17.0 %copy-start.29 = (bf16[8,256,256]{2,1,0:T(8,128)(2,1)S(1)}, bf16[8,256,256]{2,1,0:T(8,128)(2,1)}, u32[]{:S(2)}) copy-start(bf16[8,256,256]{2,1,0:T(8,128)(2,1)} %copy-done.28) | copy-start | bytes 3145732 | tf_op jit(solution)/shard_map/cond
  148.4 29.6 %all-to-all-start.2 = ((bf16[4,4,256,256]{3,2,1,0:T(8,128)(2,1)}), bf16[4,4,256,256]{3,2,1,0:T(8,128)(2,1)S(1)}, u32[]{:S(2)}, u32[]{:S(2)}) async-start(bf16[4,4,256,256]{3,2,1,0:T(8,128)(2,1)} %bitcast.19), calls=%async_computation.2 | async-start | bytes 4194304 | tf_op jit(solution)/shard_map/cond/branch_1_fun/all_to_all | solution.py:337
  152.1 13.3 %collective-permute-start.35 = (bf16[2,256,256]{2,1,0:T(8,128)(2,1)S(1)}, bf16[2,256,256]{2,1,0:T(8,128)(2,1)S(1)}, u32[]{:S(2)}, u32[]{:S(2)}) collective-permute-start(bf16[2,256,256]{2,1,0:T(8,128)(2,1)S(1)} %copy-done.44), channel_id=1, source_target_pairs={{0,24},{8,16},{16,8},{24,0},{1,25},{9,17},{17,9},{25,1},{2,26},{10... | collective-permute-start | bytes 786440 | tf_op jit(solution)/shard_map/cond/branch_1_fun/ppermute | solution.py:289
  178.0 34.5 %copy-start.23 = (bf16[4,4,256,256]{3,2,1,0:T(8,128)(2,1)}, bf16[4,4,256,256]{3,2,1,0:T(8,128)(2,1)S(1)}, u32[]{:S(2)}) copy-start(bf16[4,4,256,256]{3,2,1,0:T(8,128)(2,1)S(1)} %all-to-all-done.2.refs_0_) | copy-start | bytes 6291460 | tf_op jit(solution)/shard_map/cond
  178.0 28.9 %all-to-all-start.3 = ((bf16[4,4,256,256]{3,2,1,0:T(8,128)(2,1)}), bf16[4,4,256,256]{3,2,1,0:T(8,128)(2,1)}, u32[]{:S(2)}, u32[]{:S(2)}) async-start(bf16[4,4,256,256]{3,2,1,0:T(8,128)(2,1)} %bitcast.20), calls=%async_computation.3 | async-start | bytes 4194304 | tf_op jit(solution)/shard_map/cond/branch_1_fun/all_to_all | solution.py:337
  182.4 25.9 %collective-permute-start.36 = (bf16[4,4,256,256]{3,2,1,0:T(8,128)(2,1)S(1)}, bf16[4,4,256,256]{3,2,1,0:T(8,128)(2,1)}, u32[]{:S(2)}, u32[]{:S(2)}) collective-permute-start(bf16[4,4,256,256]{3,2,1,0:T(8,128)(2,1)S(1)} %all-to-all-done.2.refs_0_), channel_id=1, source_target_pairs={{0,1},{1,0},{2,3},{3,2},{4,5},{5,4},{6,7},{7,6},{8,9},{9,8},{10,11... | collective-permute-start | bytes 6291464 | tf_op jit(solution)/shard_map/cond/branch_1_fun/ppermute | solution.py:289
  206.9 5.6 %collective-permute-start.37 = (bf16[4,4,256,256]{3,2,1,0:T(8,128)(2,1)}, bf16[4,4,256,256]{3,2,1,0:T(8,128)(2,1)}, u32[]{:S(2)}, u32[]{:S(2)}) collective-permute-start(bf16[4,4,256,256]{3,2,1,0:T(8,128)(2,1)} %all-to-all-done.3.refs_1_), channel_id=1, source_target_pairs={{0,1},{1,0},{2,3},{3,2},{4,5},{5,4},{6,7},{7,6},{8,9},{9,8},{10,11... | collective-permute-start | bytes 6291464 | tf_op jit(solution)/shard_map/cond/branch_1_fun/ppermute | solution.py:289
  (2 other events, 1.7 us)
